TPU v7x, 128 devices: a whole 4x4x4 slice. The times are simulated.
128 devices in a mesh: dp: 4 (over z), seq: 8 (over x, core), mp: 4 (over y).
Axes of the slice: x: 4, y: 4, z: 4, core: 2. Of those that a mesh axis runs over, the one named last changes fastest.
Arguments:
- tokens: float32 [4, 4096, 1024], P('dp', 'seq'), may hold values from -6 to 6
- cotangent: float32 [4, 4096, 1024], P('dp', 'seq'), may hold values from -6 to 6
- in_weight: float32 [3, 1024, 1024], P(None, ('dp', 'seq'), 'mp'), may hold values from -0.1875 to 0.1875
- in_first: float32 [3, 1024, 1024], P(None, ('dp', 'seq'), 'mp'), may hold values from -80 to 80
- in_second: float32 [3, 1024, 1024], P(None, ('dp', 'seq'), 'mp'), may hold values from 425.984 to 6881.28
- out_weight: float32 [1024, 1024], P('mp', ('dp', 'seq')), may hold values from -0.1875 to 0.1875
- out_first: float32 [1024, 1024], P('mp', ('dp', 'seq')), may hold values from -80 to 80
- out_second: float32 [1024, 1024], P('mp', ('dp', 'seq')), may hold values from 425.984 to 6881.28
- gu_weight: float32 [2, 1024, 4608], P(None, ('dp', 'seq'), 'mp'), may hold values from -0.1875 to 0.1875
- gu_first: float32 [2, 1024, 4608], P(None, ('dp', 'seq'), 'mp'), may hold values from -24 to 24
- gu_second: float32 [2, 1024, 4608], P(None, ('dp', 'seq'), 'mp'), may hold values from 39.3216 to 622.592
- down_weight: float32 [4608, 1024], P('mp', ('dp', 'seq')), may hold values from -0.09375 to 0.09375
- down_first: float32 [4608, 1024], P('mp', ('dp', 'seq')), may hold values from -64 to 64
- down_second: float32 [4608, 1024], P('mp', ('dp', 'seq')), may hold values from 212.992 to 3440.64
- conv_weight: float32 [3, 1024], P(None, ('dp', 'seq')), may hold values from -3 to 3
- conv_first: float32 [3, 1024], P(None, ('dp', 'seq')), may hold values from -80 to 80
- conv_second: float32 [3, 1024], P(None, ('dp', 'seq')), may hold values from 425.984 to 6881.28
- norm_gains: float32 [2, 1024], P(None, ('dp', 'seq')), may hold values from 0.5 to 1.5
- gains_first: float32 [2, 1024], P(None, ('dp', 'seq')), may hold values from -80 to 80
- gains_second: float32 [2, 1024], P(None, ('dp', 'seq')), may hold values from 425.984 to 6881.28
Outputs:
- mixed: float32 [4, 4096, 1024], P('dp', 'seq')
- token_grad: float32 [4, 4096, 1024], P('dp', 'seq')
- in_master: float32 [3, 1024, 1024], P(None, ('dp', 'seq'), 'mp')
- in_moment: float32 [3, 1024, 1024], P(None, ('dp', 'seq'), 'mp')
- in_square: float32 [3, 1024, 1024], P(None, ('dp', 'seq'), 'mp')
- out_master: float32 [1024, 1024], P('mp', ('dp', 'seq'))
- out_moment: float32 [1024, 1024], P('mp', ('dp', 'seq'))
- out_square: float32 [1024, 1024], P('mp', ('dp', 'seq'))
- gu_master: float32 [2, 1024, 4608], P(None, ('dp', 'seq'), 'mp')
- gu_moment: float32 [2, 1024, 4608], P(None, ('dp', 'seq'), 'mp')
- gu_square: float32 [2, 1024, 4608], P(None, ('dp', 'seq'), 'mp')
- down_master: float32 [4608, 1024], P('mp', ('dp', 'seq'))
- down_moment: float32 [4608, 1024], P('mp', ('dp', 'seq'))
- down_square: float32 [4608, 1024], P('mp', ('dp', 'seq'))
- conv_master: float32 [3, 1024], P(None, ('dp', 'seq'))
- conv_moment: float32 [3, 1024], P(None, ('dp', 'seq'))
- conv_square: float32 [3, 1024], P(None, ('dp', 'seq'))
- gains_master: float32 [2, 1024], P(None, ('dp', 'seq'))
- gains_moment: float32 [2, 1024], P(None, ('dp', 'seq'))
- gains_square: float32 [2, 1024], P(None, ('dp', 'seq'))
All inputs are finite; a program needn't handle non-finite values.
Results may differ from a plain program's by a relative error of at most 0.025.
Values may be sent and summed in bfloat16 or wider, within the bound.
A program may use at most 128 MiB of HBM per device.

v0:
```python
import jax
import jax.numpy as jnp
from jax import lax
from jax.sharding import PartitionSpec as P

STEP = 10


beta_one = 0.9
beta_two = 0.95
eps_adam = 1e-08
eps_norm = 1e-05
rate_matrix = 0.05
rate_small = 0.3
decay_matrix = 0.1


def passed_along(value, axis, steps):
    count = lax.axis_size(axis)
    initial, last = (max(0, -steps), min(count, count - steps))
    return lax.ppermute(value, axis, [(source, source + steps) for source in range(initial, last)])


def rms_scale(values):
    return lax.rsqrt(jnp.mean(values * values, axis=-1, keepdims=True) + eps_norm)


def adamw(master, first, second, grad, rate, decay):
    moment = beta_one * first + (1.0 - beta_one) * grad
    square = beta_two * second + (1.0 - beta_two) * grad * grad
    moment_hat = moment / (1.0 - beta_one**STEP)
    square_hat = square / (1.0 - beta_two**STEP)
    renewed = master - rate * (moment_hat / (jnp.sqrt(square_hat) + eps_adam) + decay * master)
    return (renewed, moment, square)


def local(
    tokens,
    cotangent,
    in_weight,
    in_first,
    in_second,
    out_weight,
    out_first,
    out_second,
    gu_weight,
    gu_first,
    gu_second,
    down_weight,
    down_first,
    down_second,
    conv_weight,
    conv_first,
    conv_second,
    norm_gains,
    gains_first,
    gains_second,
):
    bf16 = jnp.bfloat16
    f32 = jnp.float32
    in_full, out_full, gu_full, down_full, conv_full, gains_full = (
        lax.all_gather(in_weight.astype(bf16), ("dp", "seq"), axis=1, tiled=True),
        lax.all_gather(out_weight.astype(bf16), ("dp", "seq"), axis=1, tiled=True),
        lax.all_gather(gu_weight.astype(bf16), ("dp", "seq"), axis=1, tiled=True),
        lax.all_gather(down_weight.astype(bf16), ("dp", "seq"), axis=1, tiled=True),
        lax.all_gather(conv_weight.astype(bf16), ("dp", "seq"), axis=1, tiled=True),
        lax.all_gather(norm_gains.astype(bf16), ("dp", "seq"), axis=1, tiled=True),
    )
    seqs_here, length, width = tokens.shape
    rows = seqs_here * length
    channels = in_full.shape[2]
    offset = lax.axis_index("mp") * channels
    taps = lax.dynamic_slice_in_dim(conv_full, offset, channels, 1).astype(f32)
    gain_one = gains_full[0].astype(f32)
    gain_two = gains_full[1].astype(f32)
    flat = tokens.reshape(rows, width)
    scale_one = rms_scale(flat)
    normed_one = flat * scale_one
    act_one = (normed_one * gain_one).astype(bf16)
    bgate = jnp.dot(act_one, in_full[0], preferred_element_type=f32)
    cgate = jnp.dot(act_one, in_full[1], preferred_element_type=f32)
    xvalue = jnp.dot(act_one, in_full[2], preferred_element_type=f32)
    mixed_in = (bgate * xvalue).astype(bf16).reshape(seqs_here, length, channels)
    before = passed_along(mixed_in[:, length - 2 :], "seq", 1)
    extended = jnp.concatenate([before, mixed_in], axis=1).astype(f32)
    conv_out = (
        taps[0] * extended[:, :length]
        + taps[1] * extended[:, 1 : length + 1]
        + taps[2] * extended[:, 2:]
    )
    conv_out = conv_out.reshape(rows, channels)
    gated = (cgate * conv_out).astype(bf16)
    branch = lax.psum(jnp.dot(gated, out_full, preferred_element_type=f32), "mp")
    resid = flat + branch
    scale_two = rms_scale(resid)
    normed_two = resid * scale_two
    act_two = (normed_two * gain_two).astype(bf16)
    gate_pre = jnp.dot(act_two, gu_full[0], preferred_element_type=f32)
    up_pre = jnp.dot(act_two, gu_full[1], preferred_element_type=f32)
    sigmoid_gate = jax.nn.sigmoid(gate_pre)
    swish = gate_pre * sigmoid_gate
    hidden = (swish * up_pre).astype(bf16)
    ffn = lax.psum(
        jnp.dot(hidden, down_full, preferred_element_type=f32).astype(jnp.bfloat16), "mp"
    ).astype(jnp.float32)
    mixed = (resid + ffn).reshape(tokens.shape)
    upstream = cotangent.reshape(rows, width)
    up_low = upstream.astype(bf16)
    grad_down = jnp.einsum("tf,td->fd", hidden, up_low, preferred_element_type=f32)
    grad_hidden = jnp.einsum("td,fd->tf", up_low, down_full, preferred_element_type=f32)
    grad_gate = (
        grad_hidden * up_pre * sigmoid_gate * (1.0 + gate_pre * (1.0 - sigmoid_gate))
    ).astype(bf16)
    grad_up = (grad_hidden * swish).astype(bf16)
    grad_gu = jnp.stack(
        [
            jnp.einsum("td,tf->df", act_two, grad_gate, preferred_element_type=f32),
            jnp.einsum("td,tf->df", act_two, grad_up, preferred_element_type=f32),
        ]
    )
    back_two = jnp.einsum("tf,df->td", grad_gate, gu_full[0], preferred_element_type=f32)
    back_two = back_two + jnp.einsum("tf,df->td", grad_up, gu_full[1], preferred_element_type=f32)
    back_two = lax.psum(back_two.astype(jnp.bfloat16), "mp").astype(jnp.float32)
    gains_two = jnp.sum(back_two * normed_two, axis=0)
    scaled_two = back_two * gain_two
    grad_resid = upstream + scale_two * (
        scaled_two - normed_two * jnp.mean(scaled_two * normed_two, axis=-1, keepdims=True)
    )
    resid_low = grad_resid.astype(bf16)
    grad_out = jnp.einsum("tc,td->cd", gated, resid_low, preferred_element_type=f32)
    grad_gated = jnp.einsum("td,cd->tc", resid_low, out_full, preferred_element_type=f32)
    grad_conv = (grad_gated * cgate).astype(bf16).reshape(seqs_here, length, channels)
    grad_cgate = (grad_gated * conv_out).astype(bf16)
    after = passed_along(grad_conv[:, :2], "seq", -1)
    ext_back = jnp.concatenate([grad_conv, after], axis=1).astype(f32)
    grad_mixed = (
        taps[2] * ext_back[:, :length]
        + taps[1] * ext_back[:, 1 : length + 1]
        + taps[0] * ext_back[:, 2:]
    )
    grad_mixed = grad_mixed.reshape(rows, channels)
    conv_values = ext_back[:, :length]
    grad_taps = jnp.stack(
        [
            jnp.sum(conv_values * extended[:, shift_by : shift_by + length], axis=(0, 1))
            for shift_by in range(3)
        ]
    )
    grad_bgate = (grad_mixed * xvalue).astype(bf16)
    grad_xvalue = (grad_mixed * bgate).astype(bf16)
    grad_in = jnp.stack(
        [
            jnp.einsum("td,tc->dc", act_one, grad_bgate, preferred_element_type=f32),
            jnp.einsum("td,tc->dc", act_one, grad_cgate, preferred_element_type=f32),
            jnp.einsum("td,tc->dc", act_one, grad_xvalue, preferred_element_type=f32),
        ]
    )
    back_one = jnp.einsum("tc,dc->td", grad_bgate, in_full[0], preferred_element_type=f32)
    back_one = back_one + jnp.einsum(
        "tc,dc->td", grad_cgate, in_full[1], preferred_element_type=f32
    )
    back_one = back_one + jnp.einsum(
        "tc,dc->td", grad_xvalue, in_full[2], preferred_element_type=f32
    )
    taps_padded = lax.dynamic_update_slice_in_dim(jnp.zeros((3, width), f32), grad_taps, offset, 1)
    back_one, taps_full = (
        lax.psum(back_one.astype(jnp.bfloat16), "mp").astype(jnp.float32),
        lax.psum(taps_padded.astype(jnp.bfloat16), "mp").astype(jnp.float32),
    )
    gains_one = jnp.sum(back_one * normed_one, axis=0)
    scaled_one = back_one * gain_one
    token_grad = grad_resid + scale_one * (
        scaled_one - normed_one * jnp.mean(scaled_one * normed_one, axis=-1, keepdims=True)
    )
    token_grad = token_grad.reshape(tokens.shape)
    grad_gains = jnp.stack([gains_one, gains_two])
    in_reduced, out_reduced, gu_reduced, down_reduced, conv_reduced, gains_reduced = (
        lax.psum_scatter(
            grad_in.astype(jnp.bfloat16), ("dp", "seq"), scatter_dimension=1, tiled=True
        ).astype(jnp.float32),
        lax.psum_scatter(
            grad_out.astype(jnp.bfloat16), ("dp", "seq"), scatter_dimension=1, tiled=True
        ).astype(jnp.float32),
        lax.psum_scatter(
            grad_gu.astype(jnp.bfloat16), ("dp", "seq"), scatter_dimension=1, tiled=True
        ).astype(jnp.float32),
        lax.psum_scatter(
            grad_down.astype(jnp.bfloat16), ("dp", "seq"), scatter_dimension=1, tiled=True
        ).astype(jnp.float32),
        lax.psum_scatter(
            taps_full.astype(jnp.bfloat16), ("dp", "seq"), scatter_dimension=1, tiled=True
        ).astype(jnp.float32),
        lax.psum_scatter(
            grad_gains.astype(jnp.bfloat16), ("dp", "seq"), scatter_dimension=1, tiled=True
        ).astype(jnp.float32),
    )
    in_new = adamw(in_weight, in_first, in_second, in_reduced, rate_matrix, decay_matrix)
    out_new = adamw(out_weight, out_first, out_second, out_reduced, rate_matrix, decay_matrix)
    gu_new = adamw(gu_weight, gu_first, gu_second, gu_reduced, rate_matrix, decay_matrix)
    down_new = adamw(down_weight, down_first, down_second, down_reduced, rate_matrix, decay_matrix)
    conv_new = adamw(conv_weight, conv_first, conv_second, conv_reduced, rate_small, 0.0)
    gains_new = adamw(norm_gains, gains_first, gains_second, gains_reduced, rate_small, 0.0)
    return (
        mixed,
        token_grad,
        in_new[0],
        in_new[1],
        in_new[2],
        out_new[0],
        out_new[1],
        out_new[2],
        gu_new[0],
        gu_new[1],
        gu_new[2],
        down_new[0],
        down_new[1],
        down_new[2],
        conv_new[0],
        conv_new[1],
        conv_new[2],
        gains_new[0],
        gains_new[1],
        gains_new[2],
    )


def solution(mesh):
    placed = (
        P("dp", "seq", None),
        P("dp", "seq", None),
        P(None, ("dp", "seq"), "mp"),
        P(None, ("dp", "seq"), "mp"),
        P(None, ("dp", "seq"), "mp"),
        P("mp", ("dp", "seq")),
        P("mp", ("dp", "seq")),
        P("mp", ("dp", "seq")),
        P(None, ("dp", "seq"), "mp"),
        P(None, ("dp", "seq"), "mp"),
        P(None, ("dp", "seq"), "mp"),
        P("mp", ("dp", "seq")),
        P("mp", ("dp", "seq")),
        P("mp", ("dp", "seq")),
        P(None, ("dp", "seq")),
        P(None, ("dp", "seq")),
        P(None, ("dp", "seq")),
        P(None, ("dp", "seq")),
        P(None, ("dp", "seq")),
        P(None, ("dp", "seq")),
    )
    return jax.shard_map(
        local,
        mesh=mesh,
        in_specs=placed,
        out_specs=(
            P("dp", "seq", None),
            P("dp", "seq", None),
            P(None, ("dp", "seq"), "mp"),
            P(None, ("dp", "seq"), "mp"),
            P(None, ("dp", "seq"), "mp"),
            P("mp", ("dp", "seq")),
            P("mp", ("dp", "seq")),
            P("mp", ("dp", "seq")),
            P(None, ("dp", "seq"), "mp"),
            P(None, ("dp", "seq"), "mp"),
            P(None, ("dp", "seq"), "mp"),
            P("mp", ("dp", "seq")),
            P("mp", ("dp", "seq")),
            P("mp", ("dp", "seq")),
            P(None, ("dp", "seq")),
            P(None, ("dp", "seq")),
            P(None, ("dp", "seq")),
            P(None, ("dp", "seq")),
            P(None, ("dp", "seq")),
            P(None, ("dp", "seq")),
        ),
        check_vma=False,
    )
```

profile of v0, /device:TPU:0, one launch (start us, length us, event | category | flops | bytes accessed | tf_op | source)
XLA Modules:
  0.0 881.2 jit_solution(3197970117237126267)
XLA Ops:
  9.7 22.8 %all-gather = bf16[32,32,2]{1,2,0:T(2,128)(2,1)S(1)} all-gather(bf16[1,32,2]{1,2,0:T(2,128)(2,1)S(1)} %convert_bitcast_fusion.2), channel_id=1, replica_groups=mesh['dp'=4,'seq'=8,'mp'=4] {'dp','seq'}, dimensions={0}, use_global_device_ids=true | all-gather | bytes 4224 | tf_op jit(solution)/shard_map/all_gather | solution.py:67
  33.3 22.9 %all-gather.1 = bf16[32,32,3]{1,2,0:T(4,128)(2,1)S(1)} all-gather(bf16[1,32,3]{1,2,0:T(4,128)(2,1)S(1)} %convert_bitcast_fusion.1), channel_id=1, replica_groups=mesh['dp'=4,'seq'=8,'mp'=4] {'dp','seq'}, dimensions={0}, use_global_device_ids=true | all-gather | bytes 6336 | tf_op jit(solution)/shard_map/all_gather | solution.py:66
  63.9 23.2 %all_gather.21 = bf16[256,1024]{0,1:T(8,128)(2,1)S(1)} all-gather(bf16[256,32]{0,1:T(8,128)(2,1)S(1)} %convert_element_type.152), channel_id=1, replica_groups=mesh['dp'=4,'seq'=8,'mp'=4] {'dp','seq'}, dimensions={1}, use_global_device_ids=true | all-gather | bytes 540672 | tf_op jit(solution)/shard_map/all_gather | solution.py:63
  94.8 55.0 %all-reduce.5.cloned.1.call-done = f32[512,1024]{1,0:T(8,128)} async-done(((f32[512,1024]{1,0:T(8,128)}), f32[512,1024]{1,0:T(8,128)}) %all-reduce.5.cloned.1.call-update) | async-done | bytes 2097168 | tf_op jit(solution)/shard_map/psum | solution.py:93
  154.3 45.4 %all-gather.8.cloned.1.call-done = bf16[2,1024,1152]{2,1,0:T(8,128)(2,1)} async-done(((bf16[2,32,1152]{2,1,0:T(8,128)(2,1)}), bf16[2,1024,1152]{2,1,0:T(8,128)(2,1)}) %all-gather.8.cloned.1.call-update) | async-done | bytes 4718608 | tf_op jit(solution)/shard_map/all_gather | solution.py:64
  199.8 5.1 fusion.18
  207.8 38.5 %all-gather.10.cloned.1.call-done = bf16[1152,1024]{0,1:T(8,128)(2,1)} async-done(((bf16[1152,32]{0,1:T(8,128)(2,1)}), bf16[1152,1024]{0,1:T(8,128)(2,1)}) %all-gather.10.cloned.1.call-update) | async-done | bytes 2359312 | tf_op jit(solution)/shard_map/all_gather | solution.py:65
  246.3 6.8 multiply_convert_fusion
  253.2 4.1 fusion.17
  257.2 4.2 add_convert_fusion.1
  261.7 4.6 convolution_convert_fusion.3
  266.3 40.4 %all-reduce.7.cloned.1.call-done = bf16[512,1024]{1,0:T(8,128)(2,1)} async-done(((bf16[512,1024]{1,0:T(8,128)(2,1)}), bf16[512,1024]{1,0:T(8,128)(2,1)}) %all-reduce.7.cloned.1.call-update) | async-done | bytes 1048592 | tf_op jit(solution)/shard_map/psum | solution.py:123
  321.3 3.1 convolution_convert_fusion.4
  324.4 56.6 %all-reduce.9.cloned.1.call-done = (bf16[512,1024]{1,0:T(8,128)(2,1)}, bf16[512,1024]{1,0:T(8,128)(2,1)}) async-done(((bf16[512,1024]{1,0:T(8,128)(2,1)}, bf16[512,1024]{1,0:T(8,128)(2,1)}), (bf16[512,1024]{1,0:T(8,128)(2,1)}, bf16[512,1024]{1,0:T(8,128)(2,1)})) %all-reduce.9.cloned.1.call-update) | async-done | bytes 2097168 | tf_op jit(solution)/shard_map/psum | solution.py:103
  384.0 5.0 fusion.70
  393.3 2.9 fusion
  400.6 61.0 %reduce-scatter.21.cloned.1.call-done = bf16[32,3]{1,0:T(8,128)(2,1)} async-done(((bf16[1024,3]{1,0:T(8,128)(2,1)}), bf16[32,3]{1,0:T(8,128)(2,1)}) %reduce-scatter.21.cloned.1.call-update) | async-done | bytes 208
  463.0 11.2 %psum.40 = bf16[3,32]{1,0:T(4,128)(2,1)} all-reduce(bf16[3,32]{1,0:T(4,128)(2,1)} %copy.47), channel_id=1, replica_groups=mesh['dp'=4,'seq'=8,'mp'=4] {'mp'}, use_global_device_ids=true, to_apply=%region_15.0 | all-reduce | flops 96 | bytes 384 | tf_op jit(solution)/shard_map/psum | solution.py:168
  475.4 66.4 %reduce-scatter.13.cloned.1.call-done = bf16[256,32]{0,1:T(8,128)(2,1)} async-done(((bf16[256,1024]{0,1:T(8,128)(2,1)}), bf16[256,32]{0,1:T(8,128)(2,1)}) %reduce-scatter.13.cloned.1.call-update) | async-done | bytes 16400 | tf_op jit(solution)/shard_map/reduce_scatter | solution.py:181
  543.2 5.1 fusion.10
  548.3 73.6 %reduce-scatter.19.cloned.1.call-done = bf16[32,2]{1,0:T(8,128)(2,1)} async-done(((bf16[1024,2]{1,0:T(8,128)(2,1)}), bf16[32,2]{1,0:T(8,128)(2,1)}) %reduce-scatter.19.cloned.1.call-update) | async-done | bytes 144
  624.0 80.3 %reduce-scatter.17.cloned.1.call-done = bf16[1152,32]{0,1:T(8,128)(2,1)} async-done(((bf16[1152,1024]{0,1:T(8,128)(2,1)}), bf16[1152,32]{0,1:T(8,128)(2,1)}) %reduce-scatter.17.cloned.1.call-update) | async-done | bytes 73744 | tf_op jit(solution)/shard_map/reduce_scatter | solution.py:187
  706.3 79.3 %reduce-scatter.11.cloned.1.call-done = bf16[3,32,256]{2,1,0:T(8,128)(2,1)} async-done(((bf16[3,1024,256]{2,1,0:T(8,128)(2,1)}), bf16[3,32,256]{2,1,0:T(8,128)(2,1)}) %reduce-scatter.11.cloned.1.call-update) | async-done | bytes 49168 | tf_op jit(solution)/shard_map/reduce_scatter | solution.py:178
  787.3 85.0 %reduce-scatter.15.cloned.1.call-done = bf16[2,32,1152]{2,1,0:T(8,128)(2,1)} async-done(((bf16[2,1024,1152]{2,1,0:T(8,128)(2,1)}), bf16[2,32,1152]{2,1,0:T(8,128)(2,1)}) %reduce-scatter.15.cloned.1.call-update) | async-done | bytes 147472 | tf_op jit(solution)/shard_map/reduce_scatter | solution.py:184
  (168 shorter events, 63.9 us)
Async XLA Ops:
  7.2 52.0 %all-gather.6.cloned.1.call-start = ((), (), s32[]{:S(2)}) async-start(), calls=%async_computation.6 | async-start | bytes 1622016 | tf_op jit(solution)/shard_map/all_gather | solution.py:62
  8.9 140.9 %all-reduce.5.cloned.1.call-start = ((), (), s32[]{:S(2)}) async-start(), calls=%async_computation.7 | async-start | bytes 4194304 | tf_op jit(solution)/shard_map/psum | solution.py:93
  58.8 322.1 %copy-start.30 = (f32[512]{0:T(512)}, f32[512]{0:T(512)S(1)}, u32[]{:S(2)}) copy-start(f32[512]{0:T(512)S(1)} %add_rsqrt_fusion.1) | copy-start | bytes 6148
  58.9 322.1 %copy-start.26 = (f32[1,1024]{1,0:T(1,128)}, f32[1,1024]{1,0:T(1,128)S(1)}, u32[]{:S(2)}) copy-start(f32[1,1024]{1,0:T(1,128)S(1)} %get-tuple-element.60) | copy-start | bytes 12292
  61.7 25.4 %collective-permute-start = (bf16[1,2,256]{2,1,0:T(2,128)(2,1)S(1)}, bf16[1,2,256]{2,1,0:T(2,128)(2,1)S(1)}, u32[]{:S(2)}, u32[]{:S(2)}) collective-permute-start(bf16[1,2,256]{2,1,0:T(2,128)(2,1)S(1)} %slice.89), channel_id=1, source_target_pairs={{0,4},{4,8},{8,12},{12,16},{16,20},{20,24},{24,28},{1,5},{5,9},{9,... | collective-permute-start | bytes 3080 | tf_op jit(solution)/shard_map/ppermute | solution.py:21
  92.4 107.4 %all-gather.8.cloned.1.call-start = ((), (), s32[]{:S(2)}) async-start(), calls=%async_computation.8 | async-start | bytes 4866048 | tf_op jit(solution)/shard_map/all_gather | solution.py:64
  93.2 153.2 %all-gather.10.cloned.1.call-start = ((), (), s32[]{:S(2)}) async-start(), calls=%async_computation.9 | async-start | bytes 2433024 | tf_op jit(solution)/shard_map/all_gather | solution.py:65
  94.8 211.9 %all-reduce.7.cloned.1.call-start = ((), (), s32[]{:S(2)}) async-start(), calls=%async_computation.10 | async-start | bytes 2097152 | tf_op jit(solution)/shard_map/psum | solution.py:123
  261.5 119.5 %all-reduce.9.cloned.1.call-start = ((), (), s32[]{:S(2)}) async-start(), calls=%async_computation.17 | async-start | bytes 4194304 | tf_op jit(solution)/shard_map/psum | solution.py:103
  313.8 3.2 collective-permute-start.1
  320.0 141.6 %reduce-scatter.21.cloned.1.call-start = ((), (), s32[]{:S(2)}) async-start(), calls=%async_computation.16 | async-start | bytes 270336
  321.2 220.6 %reduce-scatter.13.cloned.1.call-start = ((), (), s32[]{:S(2)}) async-start(), calls=%async_computation.12 | async-start | bytes 540672 | tf_op jit(solution)/shard_map/reduce_scatter | solution.py:181
  324.3 297.6 %reduce-scatter.19.cloned.1.call-start = ((), (), s32[]{:S(2)}) async-start(), calls=%async_computation.15 | async-start | bytes 270336
  384.0 320.4 %reduce-scatter.17.cloned.1.call-start = ((), (), s32[]{:S(2)}) async-start(), calls=%async_computation.14 | async-start | bytes 2433024 | tf_op jit(solution)/shard_map/reduce_scatter | solution.py:187
  389.0 396.5 %reduce-scatter.11.cloned.1.call-start = ((), (), s32[]{:S(2)}) async-start(), calls=%async_computation.11 | async-start | bytes 1622016 | tf_op jit(solution)/shard_map/reduce_scatter | solution.py:178
  393.0 479.2 %reduce-scatter.15.cloned.1.call-start = ((), (), s32[]{:S(2)}) async-start(), calls=%async_computation.13 | async-start | bytes 4866048 | tf_op jit(solution)/shard_map/reduce_scatter | solution.py:184
  400.5 141.3 %copy-start.25 = (f32[256,32]{0,1:T(8,128)S(1)}, f32[256,32]{0,1:T(8,128)}, u32[]{:S(2)}) copy-start(f32[256,32]{0,1:T(8,128)} %param.25) | copy-start | bytes 98308
  400.5 141.3 %copy-start.28 = (f32[256,32]{0,1:T(8,128)S(1)}, f32[256,32]{0,1:T(8,128)}, u32[]{:S(2)}) copy-start(f32[256,32]{0,1:T(8,128)} %param.26) | copy-start | bytes 98308
  400.5 141.3 %copy-start.29 = (f32[256,32]{0,1:T(8,128)S(1)}, f32[256,32]{0,1:T(8,128)}, u32[]{:S(2)}) copy-start(f32[256,32]{0,1:T(8,128)} %param.27) | copy-start | bytes 98308
  400.5 142.7 %copy-start.5 = (bf16[512,1024]{1,0:T(8,128)(2,1)S(1)}, bf16[512,1024]{1,0:T(8,128)(2,1)}, u32[]{:S(2)}) copy-start(bf16[512,1024]{1,0:T(8,128)(2,1)} %get-tuple-element.28) | copy-start | bytes 3145732
  400.5 142.7 %copy-start.27 = (f32[1,1024]{1,0:T(1,128)S(1)}, f32[1,1024]{1,0:T(1,128)}, u32[]{:S(2)}) copy-start(f32[1,1024]{1,0:T(1,128)} %copy-done.26) | copy-start | bytes 12292
  400.5 142.7 %copy-start.31 = (f32[512]{0:T(512)S(1)}, f32[512]{0:T(512)}, u32[]{:S(2)}) copy-start(f32[512]{0:T(512)} %copy-done.30) | copy-start | bytes 6148
  543.2 79.5 %copy-start.33 = (f32[2,32]{1,0:T(2,128)S(1)}, f32[2,32]{1,0:T(2,128)}, u32[]{:S(2)}) copy-start(f32[2,32]{1,0:T(2,128)} %param.37) | copy-start | bytes 772
  543.2 242.3 %copy-start.24 = (f32[3,32,256]{2,1,0:T(8,128)S(1)}, f32[3,32,256]{2,1,0:T(8,128)}, u32[]{:S(2)}) copy-start(f32[3,32,256]{2,1,0:T(8,128)} %param.22) | copy-start | bytes 294916
  (28 other events, 236.6 us)
Sparse Core Ops, SparseCore 0:
  10.9 45.8 all-gather.5
  92.5 57.3 all-reduce.4
  153.0 46.7 all-gather.7
  202.7 43.5 all-gather.9
  261.6 45.0 all-reduce.6
  320.2 60.7 all-reduce.8
  384.8 76.7 reduce-scatter.20
  465.4 76.3 reduce-scatter.12
  545.7 76.2 reduce-scatter.18
  625.8 78.5 reduce-scatter.16
  707.9 77.5 reduce-scatter.10
  789.1 83.0 reduce-scatter.14
where the time goes:
time: 882 us; the launch traced here: 881 us
  waiting for transfers between devices  683 us (77%)
  blocking collectives  80 us (9%)
  matrix products  52.3 us (6%)
  other arithmetic  37.9 us (4%)
  between operations  14.8 us (2%)
    unnamed x14, waiting for transfers between devices  135 us
    reduce_scatter x1, waiting for transfers between devices, local(): lax.psum_scatter(grad_gu.astype(jnp.bfloat16), ('dp', 'seq'), scatter_dim...  85 us
    reduce_scatter x1, waiting for transfers between devices, local(): lax.psum_scatter(grad_down.astype(jnp.bfloat16), ('dp', 'seq'), scatter_d...  80.3 us
    reduce_scatter x1, waiting for transfers between devices, local(): lax.psum_scatter(grad_in.astype(jnp.bfloat16), ('dp', 'seq'), scatter_dim...  79.3 us
    reduce_scatter x1, waiting for transfers between devices, local(): lax.psum_scatter(grad_out.astype(jnp.bfloat16), ('dp', 'seq'), scatter_di...  66.4 us
    psum x1, waiting for transfers between devices, local(): lax.psum(jnp.dot(hidden, down_full, preferred_element_type=f32).astype(jn...  56.6 us
    psum x1, waiting for transfers between devices, local(): lax.psum(jnp.dot(gated, out_full, preferred_element_type=f32), 'mp')  55 us
    all_gather x1, waiting for transfers between devices, local(): lax.all_gather(gu_weight.astype(bf16), ('dp', 'seq'), axis=1, tiled=True)  45.4 us
  transfers between devices with their start and end apart: 14, of which 12 were waited for; matrix products, arithmetic and copies ran while one was open for 7% of the time, Pallas kernels for 0%

commit v1 on v0

v1 whole, which is shorter than its diff:
```python
import jax
import jax.numpy as jnp
from jax import lax
from jax.experimental import pallas as pl
from jax.experimental.pallas import tpu as pltpu
from jax.sharding import PartitionSpec as P

STEP = 10

beta_one = 0.9
beta_two = 0.95
eps_adam = 1e-08
eps_norm = 1e-05
rate_matrix = 0.05
rate_small = 0.3
decay_matrix = 0.1

MESH = pl.DeviceIdType.MESH
bf16 = jnp.bfloat16
f32 = jnp.float32

ROWS = 512
CHUNK = 128
D = 1024
CH = 256
FF = 1152
IN0, OUT0, SM0, GU0, DN0, COLS = 0, 768, 1024, 1152, 3456, 4608


def adamw(master, first, second, grad, rate, decay):
    moment = beta_one * first + (1.0 - beta_one) * grad
    square = beta_two * second + (1.0 - beta_two) * grad * grad
    moment_hat = moment / (1.0 - beta_one**STEP)
    square_hat = square / (1.0 - beta_two**STEP)
    renewed = master - rate * (moment_hat / (jnp.sqrt(square_hat) + eps_adam) + decay * master)
    return (renewed, moment, square)


def rms_scale(values):
    return lax.rsqrt(jnp.mean(values * values, axis=-1, keepdims=True) + eps_norm)


def dot_nn(a, b):
    return jnp.dot(a, b, preferred_element_type=f32)


def dot_nt(a, b):
    return lax.dot_general(a, b, (((1,), (1,)), ((), ())), preferred_element_type=f32)


def dot_tn(a, b):
    return lax.dot_general(a, b, (((0,), (0,)), ((), ())), preferred_element_type=f32)


N_SEMS = 128


def kernel(
    tok_h,
    cot_h,
    w_in,
    w_out,
    w_gu,
    w_dn,
    w_conv,
    w_gain,
    mixed_o,
    tg_o,
    g_in,
    g_out,
    g_gu,
    g_dn,
    small_o,
    tok,
    cot,
    htok,
    square,
    W,
    G,
    RC,
    RX,
    T,
    RZ,
    act1,
    ulow,
    act2,
    rlow,
    hid,
    GG,
    b_s,
    c_s,
    x_s,
    conv_s,
    xext,
    gext,
    mxb,
    gated,
    GB,
    hb,
    smw,
    SM,
    SMR,
    PY,
    RY,
    OWN,
    res_s,
    mixrow,
    tgrow,
    ssem,
    rsem,
    lsem,
):
    z = lax.axis_index("dp")
    seq = lax.axis_index("seq")
    y = lax.axis_index("mp")
    x = seq // 2
    c = lax.rem(seq, 2)
    oc = 1 - c

    def near(value, step):
        return lax.rem(value + step, 4)

    def to_x(step):
        return (z, near(x, step) * 2 + c, y)

    def to_z(step):
        return (near(z, step), seq, y)

    def to_y(step):
        return (z, seq, near(y, step))

    to_core = (z, x * 2 + oc, y)
    to_next = (z, lax.rem(seq + 1, 8), y)
    to_prev = (z, lax.rem(seq + 7, 8), y)

    counter = [0]
    pending = []

    def send(src, dst, where):
        i = counter[0]
        counter[0] += 1
        copy = pltpu.make_async_remote_copy(
            src, dst, ssem.at[i], rsem.at[i], device_id=where, device_id_type=MESH
        )
        copy.start()
        pending.append(copy)
        return copy

    def arrived(copies):
        for copy in copies:
            copy.wait_recv()

    barrier = pltpu.get_barrier_semaphore()
    peers = [to_core, to_next, to_prev]
    for step in (1, 2, 3):
        peers += [to_x(step), to_z(step), to_y(step)]
    for peer in peers:
        pl.semaphore_signal(barrier, inc=1, device_id=peer, device_id_type=MESH)
    load_tok = pltpu.make_async_copy(tok_h, tok, lsem.at[2])
    load_tok.start()
    load_cot = pltpu.make_async_copy(cot_h, cot, lsem.at[3])
    load_cot.start()

    for k in range(3):
        W[z, x, c, :, CH * k : CH * k + CH] = w_in[k].astype(bf16)
    W[z, x, c, :, OUT0:SM0] = w_out[...].T.astype(bf16)
    square[...] = jnp.zeros((128, 128), f32)
    square[0:3, 0:32] = w_conv[...]
    square[3:5, 0:32] = w_gain[...]
    W[z, x, c, :, SM0:GU0] = square[...].T[0:32].astype(bf16)
    for t in range(9):
        for k in range(2):
            at = GU0 + 256 * t + 128 * k
            W[z, x, c, :, at : at + 128] = w_gu[k, :, 128 * t : 128 * t + 128].astype(bf16)
    W[z, x, c, :, DN0:COLS] = w_dn[...].T.astype(bf16)
    pl.semaphore_wait(barrier, len(peers))

    def ag_one(lo, mid, hi):
        a, b = pl.ds(lo, mid - lo), pl.ds(mid, hi - mid)
        src_a, src_b = W.at[z, x, c, :, a], W.at[z, x, c, :, b]
        return (
            [send(src_a, src_a, to_x(s)) for s in (1, 3, 2)],
            [send(src_b, src_b, to_z(s)) for s in (1, 3, 2)],
        )

    def ag_two(copies, lo, mid, hi):
        a, b = pl.ds(lo, mid - lo), pl.ds(mid, hi - mid)
        src_a, src_b = W.at[z, :, c, :, a], W.at[:, x, c, :, b]
        arrived(copies[0])
        first = [send(src_a, src_a, to_z(s)) for s in (1, 3, 2)]
        arrived(copies[1])
        return first + [send(src_b, src_b, to_x(s)) for s in (1, 3, 2)]

    def ag_three(copies, lo, hi):
        arrived(copies)
        src = W.at[:, :, c, :, pl.ds(lo, hi - lo)]
        return [send(src, src, to_core)]

    g0 = (IN0, 640, GU0)
    g1 = (GU0, GU0 + 1152, DN0)
    g2 = (DN0, DN0 + 640, COLS)
    ag0 = ag_one(*g0)
    halo = send(tok_h.at[pl.ds(ROWS - 16, 16)], htok, to_next)
    load_cot.wait()
    for r in range(0, ROWS, 128):
        ulow[r : r + 128] = cot[r : r + 128].astype(bf16)
    ag0 = ag_two(ag0, *g0)
    ag1 = ag_one(*g1)
    ag2 = ag_one(*g2)
    ag0 = ag_three(ag0, IN0, GU0)
    ag1 = ag_two(ag1, *g1)
    ag2 = ag_two(ag2, *g2)
    arrived(ag0)

    def weights(lo, n):
        return W[:, :, :, :, pl.ds(lo, n)].reshape(D, n)

    def weight_rows(block, lo, n):
        return W[block, :, :, :, pl.ds(lo, n)].reshape(256, n)

    smw[...] = weights(SM0, 128).astype(f32).T[:8]
    gain_one = smw[3:4]
    gain_two = smw[4:5]
    own_channels = pl.ds(pl.multiple_of(y * CH, CH), CH)
    taps = smw[:, own_channels]
    tap0, tap1, tap2 = taps[0:1], taps[1:2], taps[2:3]

    def first_norm(v):
        return (v * rms_scale(v) * gain_one).astype(bf16)

    load_tok.wait()
    for r in range(0, ROWS, 128):
        act1[r + 16 : r + 144] = first_norm(tok[r : r + 128])
    arrived([halo])
    act1[0:16] = first_norm(htok[...])
    bgate = dot_nn(act1[...], weights(0, CH))
    xvalue = dot_nn(act1[...], weights(2 * CH, CH))
    xext[...] = (bgate * xvalue).astype(bf16).astype(f32)
    b_s[...] = bgate[16:]
    x_s[...] = xvalue[16:]
    xext[0:16] = jnp.where(seq > 0, xext[0:16], 0.0)
    c_s[...] = dot_nn(act1[16:], weights(CH, CH))
    conv_s[...] = (
        tap0 * xext[14 : ROWS + 14] + tap1 * xext[15 : ROWS + 15] + tap2 * xext[16 : ROWS + 16]
    )
    gated[...] = (c_s[...] * conv_s[...]).astype(bf16)

    def chunk_rows(step):
        return pl.ds(pl.multiple_of(near(y, step) * CHUNK, CHUNK), CHUNK)

    def partial(which, step, values, lo, n):
        for block in range(4):
            part = dot_nt(values, weight_rows(block, lo, n))
            cols = slice(block * 256, block * 256 + 256)
            if step == 0:
                OWN[which, :, cols] = part
            else:
                PY[which, step - 1, :, cols] = part.astype(bf16)
        if step:
            return [send(PY.at[which, step - 1], RY.at[which, step - 1], to_y(step))]
        return []

    def summed(which, copies):
        arrived(copies)
        return (
            OWN[which]
            + RY[which, 0].astype(f32)
            + RY[which, 1].astype(f32)
            + RY[which, 2].astype(f32)
        )

    def ag_y(src, slot):
        return (send(src, slot(y), to_y(1)), send(src, slot(y), to_y(3)))

    def ag_y_pass(copies, slot):
        half = CHUNK // 2
        arrived(copies[:1])
        left = slot(near(y, 3)).at[pl.ds(0, half)]
        out = [send(left, left, to_y(1))]
        arrived(copies[1:])
        right = slot(near(y, 1)).at[pl.ds(half, half)]
        return out + [send(right, right, to_y(3))]

    rs = []
    for step in (2, 1, 3, 0):
        rs += partial(0, step, gated[chunk_rows(step)], OUT0, CH)

    ag1 = ag_three(ag1, GU0, DN0)
    ag2 = ag_three(ag2, DN0, COLS)

    own_rows = chunk_rows(0)
    resid = tok[own_rows] + summed(0, rs)
    res_s[...] = resid
    act2[y] = (resid * rms_scale(resid) * gain_two).astype(bf16)
    def act2_slot(i):
        return act2.at[i]

    ag_act2 = ag_y(act2.at[y], act2_slot)
    arrived(ag1)
    arrived(ag2)

    def ffn_part(acts, ups, rows, f_lo, n):
        gu = dot_nn(acts, weights(GU0 + 2 * f_lo, 2 * n))
        gh = dot_nn(ups, weights(DN0 + f_lo, n))
        for j in range(n // 128):
            gate = gu[:, 256 * j : 256 * j + 128]
            up = gu[:, 256 * j + 128 : 256 * j + 256]
            grad = gh[:, 128 * j : 128 * j + 128]
            sig = jax.nn.sigmoid(gate)
            swish = gate * sig
            hid[rows, pl.ds(f_lo + 128 * j, 128)] = (swish * up).astype(bf16)
            grad_gate = grad * up * sig * (1.0 + gate * (1.0 - sig))
            GG[rows, pl.ds(2 * f_lo + 256 * j, 128)] = grad_gate.astype(bf16)
            GG[rows, pl.ds(2 * f_lo + 256 * j + 128, 128)] = (grad * swish).astype(bf16)

    rs = []
    for step in (0, 1, 3, 2):
        if step == 1:
            ag_act2 = ag_y_pass(ag_act2, act2_slot)
        if step == 2:
            arrived(ag_act2)
        rows = chunk_rows(step)
        acts = act2[near(y, step)]
        ups = ulow[rows]

        @pl.loop(0, 4)
        def _(t):
            ffn_part(acts, ups, rows, pl.multiple_of(t * 256, 256), 256)

        ffn_part(acts, ups, rows, 1024, 128)
        rs += partial(1, step, GG[rows], GU0, 2 * FF)

    def weight_grad(left, right, lo, n):
        for block in range(4):
            values = left(block)
            for start in range(0, n, 384):
                width = min(384, n - start)
                part = dot_tn(values, right[:, pl.ds(start, width)])
                G[block, :, :, :, pl.ds(lo + start, width)] = part.astype(bf16).reshape(
                    4, 2, 32, width
                )

    def rs_core(lo, hi):
        cols = pl.ds(lo, hi - lo)
        return [send(G.at[:, :, oc, :, cols], RC.at[:, :, :, cols], to_core)]

    def rs_one(copies, lo, mid, hi):
        arrived(copies)
        cols = pl.ds(lo, hi - lo)

        @pl.loop(0, 4)
        def _(i):
            for j in range(4):
                G[i, j, c, :, cols] = (
                    G[i, j, c, :, cols].astype(f32) + RC[i, j, :, cols].astype(f32)
                ).astype(bf16)

        a, b = pl.ds(lo, mid - lo), pl.ds(mid, hi - mid)
        out = []
        for s in (1, 3, 2):
            out += [send(G.at[:, near(x, s), c, :, a], RX.at[s - 1, :, :, a], to_x(s))]
            out += [send(G.at[near(z, s), :, c, :, b], RX.at[s - 1, :, :, b], to_z(s))]
        return out

    def rs_two(copies, lo, mid, hi):
        arrived(copies)
        a, b = pl.ds(lo, mid - lo), pl.ds(mid, hi - mid)

        @pl.loop(0, 4)
        def _(i):
            T[i, :, a] = (
                G[i, x, c, :, a].astype(f32)
                + RX[0, i, :, a].astype(f32)
                + RX[1, i, :, a].astype(f32)
                + RX[2, i, :, a].astype(f32)
            ).astype(bf16)
            T[i, :, b] = (
                G[z, i, c, :, b].astype(f32)
                + RX[0, i, :, b].astype(f32)
                + RX[1, i, :, b].astype(f32)
                + RX[2, i, :, b].astype(f32)
            ).astype(bf16)

        out = []
        for s in (1, 3, 2):
            out += [send(T.at[near(z, s), :, a], RZ.at[s - 1, :, a], to_z(s))]
            out += [send(T.at[near(x, s), :, b], RZ.at[s - 1, :, b], to_x(s))]
        return out

    def rs_end(lo, n, mid):
        cols = pl.ds(lo, n)
        mine = z if lo < mid else x
        return (
            T[mine, :, cols].astype(f32)
            + RZ[0, :, cols].astype(f32)
            + RZ[1, :, cols].astype(f32)
            + RZ[2, :, cols].astype(f32)
        )

    gi = (IN0, 512, SM0)
    weight_grad(
        lambda i: act2[:, :, i * 256 : i * 256 + 256].reshape(ROWS, 256), GG, GU0, 2 * FF
    )
    r_gu = rs_core(GU0, DN0)

    back_two = summed(1, rs)
    resid = res_s[...]
    scale_two = rms_scale(resid)
    normed = resid * scale_two
    SM[0] = jnp.zeros((8, D), f32)
    SM[0, 4:5] = jnp.sum(back_two * normed, axis=0, keepdims=True)
    scaled = back_two * gain_two
    grad_resid = cot[own_rows] + scale_two * (
        scaled - normed * jnp.mean(scaled * normed, axis=-1, keepdims=True)
    )
    rlow[y] = grad_resid.astype(bf16)

    def rlow_slot(i):
        return rlow.at[i]

    ag_rlow = ag_y(rlow.at[y], rlow_slot)
    OWN[1] = grad_resid

    weight_grad(lambda i: ulow[:, i * 256 : i * 256 + 256], hid, DN0, FF)
    r_dn = rs_core(DN0, COLS)
    rs_ffn = partial(2, 2, hid[chunk_rows(2)], DN0, FF)
    r_gu = rs_one(r_gu, *g1)
    ag_rlow = ag_y_pass(ag_rlow, rlow_slot)
    for step in (1, 3, 0):
        rs_ffn += partial(2, step, hid[chunk_rows(step)], DN0, FF)
    r_dn = rs_one(r_dn, *g2)

    arrived(ag_rlow)
    low = rlow[...].reshape(ROWS, D)
    grad_gated = dot_nn(low, weights(OUT0, CH))
    gext[0:ROWS] = (grad_gated * c_s[...]).astype(bf16).astype(f32)
    mxb[...] = gext[0:16].astype(bf16)
    halo = send(mxb, hb, to_prev)
    GB[:, CH : 2 * CH] = (grad_gated * conv_s[...]).astype(bf16)
    grad_conv = gext[0:ROWS]
    for k in range(3):
        row = jnp.sum(grad_conv * xext[14 + k : ROWS + 14 + k], axis=0, keepdims=True)
        SM[0, k : k + 1, own_channels] = row
    weight_grad(
        lambda i: rlow[:, :, i * 256 : i * 256 + 256].reshape(ROWS, 256), gated, OUT0, CH
    )
    arrived([halo])
    gext[ROWS : ROWS + 8] = jnp.where(seq < 7, hb[...].astype(f32)[0:8], 0.0)
    grad_mixed = tap2 * gext[0:ROWS] + tap1 * gext[1 : ROWS + 1] + tap0 * gext[2 : ROWS + 2]
    GB[:, 0:CH] = (grad_mixed * x_s[...]).astype(bf16)
    GB[:, 2 * CH : 3 * CH] = (grad_mixed * b_s[...]).astype(bf16)

    rs = []
    for step in (2, 1, 3, 0):
        rs += partial(3, step, GB[chunk_rows(step)], IN0, 3 * CH)

    weight_grad(lambda i: act1[16:, i * 256 : i * 256 + 256], GB, IN0, 3 * CH)
    r_in = rs_core(IN0, SM0)
    r_gu = rs_two(r_gu, *g1)
    r_dn = rs_two(r_dn, *g2)

    mixrow[...] = (res_s[...] + summed(2, rs_ffn)).astype(bf16)

    def mixed_slot(i):
        return mixed_o.at[i]

    ag_mixed = ag_y(mixrow, mixed_slot)
    local_mixed = pltpu.make_async_copy(mixrow, mixed_o.at[y], lsem.at[0])
    local_mixed.start()
    r_in = rs_one(r_in, *gi)

    back_one = summed(3, rs)
    own_tok = tok[own_rows]
    scale_one = rms_scale(own_tok)
    normed = own_tok * scale_one
    SM[0, 3:4] = jnp.sum(back_one * normed, axis=0, keepdims=True)
    scaled = back_one * gain_one
    tgrow[...] = (
        OWN[1]
        + scale_one * (scaled - normed * jnp.mean(scaled * normed, axis=-1, keepdims=True))
    ).astype(bf16)

    def tg_slot(i):
        return tg_o.at[i]

    ag_tg = ag_y(tgrow, tg_slot)
    local_tg = pltpu.make_async_copy(tgrow, tg_o.at[y], lsem.at[1])
    local_tg.start()

    sm = [send(SM.at[0], SMR.at[0], to_core)]
    ag_mixed = ag_y_pass(ag_mixed, mixed_slot)
    arrived(sm)
    SM[1] = SM[0] + SMR[0]
    sm = [send(SM.at[1], SMR.at[s], to_x(s)) for s in (1, 3, 2)]

    arrived(r_dn)
    g_dn[:, 0:640] = rs_end(DN0, 640, g2[1])
    g_dn[:, 640:1152] = rs_end(DN0 + 640, 512, g2[1])

    r_in = rs_two(r_in, *gi)
    arrived(sm)
    SM[2] = SM[1] + SMR[1] + SMR[2] + SMR[3]
    sm = [send(SM.at[2], SMR.at[3 + s], to_z(s)) for s in (1, 3, 2)]

    ag_tg = ag_y_pass(ag_tg, tg_slot)
    arrived(r_gu)
    for t in range(9):
        g_gu[0, :, 128 * t : 128 * t + 128] = rs_end(GU0 + 256 * t, 128, g1[1])
        g_gu[1, :, 128 * t : 128 * t + 128] = rs_end(GU0 + 256 * t + 128, 128, g1[1])

    arrived(sm)
    SMR[7] = SM[2] + SMR[4] + SMR[5] + SMR[6]
    sm = [send(SMR.at[7], SMR.at[7 + s], to_y(s)) for s in (1, 3, 2)]

    arrived(r_in)
    for k in range(3):
        g_in[k] = rs_end(IN0 + CH * k, CH, gi[1])
    g_out[...] = rs_end(OUT0, CH, gi[1])

    arrived(sm)

    def term(j):
        return SMR[7 + lax.rem(y - j + 4, 4)]

    small_o[...] = ((term(0) + term(1)) + term(2)) + term(3)

    arrived(ag_mixed)
    arrived(ag_tg)
    local_mixed.wait()
    local_tg.wait()
    for copy in pending:
        copy.wait_send()


def local(
    tokens,
    cotangent,
    in_weight,
    in_first,
    in_second,
    out_weight,
    out_first,
    out_second,
    gu_weight,
    gu_first,
    gu_second,
    down_weight,
    down_first,
    down_second,
    conv_weight,
    conv_first,
    conv_second,
    norm_gains,
    gains_first,
    gains_second,
):
    vmem = pl.BlockSpec(memory_space=pltpu.VMEM)
    hbm = pl.BlockSpec(memory_space=pl.ANY)
    shape = jax.ShapeDtypeStruct
    mixed, tg, grad_in, grad_out, grad_gu, grad_dn, grad_small = pl.pallas_call(
        kernel,
        out_shape=(
            shape((4, CHUNK, D), bf16),
            shape((4, CHUNK, D), bf16),
            shape((3, 32, CH), f32),
            shape((32, CH), f32),
            shape((2, 32, FF), f32),
            shape((32, FF), f32),
            shape((8, D), f32),
        ),
        in_specs=[hbm] * 2 + [vmem] * 6,
        out_specs=(hbm, hbm, vmem, vmem, vmem, vmem, vmem),
        scratch_shapes=[
            pltpu.VMEM((ROWS, D), f32),
            pltpu.VMEM((ROWS, D), f32),
            pltpu.VMEM((16, D), f32),
            pltpu.VMEM((128, 128), f32),
            pltpu.VMEM((4, 4, 2, 32, COLS), bf16),
            pltpu.VMEM((4, 4, 2, 32, COLS), bf16),
            pltpu.VMEM((4, 4, 32, COLS), bf16),
            pltpu.VMEM((3, 4, 32, COLS), bf16),
            pltpu.VMEM((4, 32, COLS), bf16),
            pltpu.VMEM((3, 32, COLS), bf16),
            pltpu.VMEM((ROWS + 16, D), bf16),
            pltpu.VMEM((ROWS, D), bf16),
            pltpu.VMEM((4, CHUNK, D), bf16),
            pltpu.VMEM((4, CHUNK, D), bf16),
            pltpu.VMEM((ROWS, FF), bf16),
            pltpu.VMEM((ROWS, 2 * FF), bf16),
            pltpu.VMEM((ROWS, CH), f32),
            pltpu.VMEM((ROWS, CH), f32),
            pltpu.VMEM((ROWS, CH), f32),
            pltpu.VMEM((ROWS, CH), f32),
            pltpu.VMEM((ROWS + 16, CH), f32),
            pltpu.VMEM((ROWS + 8, CH), f32),
            pltpu.VMEM((16, CH), bf16),
            pltpu.VMEM((ROWS, CH), bf16),
            pltpu.VMEM((ROWS, 3 * CH), bf16),
            pltpu.VMEM((16, CH), bf16),
            pltpu.VMEM((8, D), f32),
            pltpu.VMEM((3, 8, D), f32),
            pltpu.VMEM((11, 8, D), f32),
            pltpu.VMEM((4, 3, CHUNK, D), bf16),
            pltpu.VMEM((4, 3, CHUNK, D), bf16),
            pltpu.VMEM((4, CHUNK, D), f32),
            pltpu.VMEM((CHUNK, D), f32),
            pltpu.VMEM((CHUNK, D), bf16),
            pltpu.VMEM((CHUNK, D), bf16),
            pltpu.SemaphoreType.DMA((N_SEMS,)),
            pltpu.SemaphoreType.DMA((N_SEMS,)),
            pltpu.SemaphoreType.DMA((4,)),
        ],
        name="block_step",
        compiler_params=pltpu.CompilerParams(
            collective_id=0, has_side_effects=True, vmem_limit_bytes=62 << 20
        ),
    )(
        tokens.reshape(ROWS, D),
        cotangent.reshape(ROWS, D),
        in_weight,
        out_weight,
        gu_weight,
        down_weight,
        conv_weight,
        norm_gains,
    )
    here = (lax.axis_index("dp") * 8 + lax.axis_index("seq")) * 32
    conv_grad = lax.dynamic_slice(grad_small, (0, here), (3, 32))
    gains_grad = lax.dynamic_slice(grad_small, (3, here), (2, 32))
    in_new = adamw(in_weight, in_first, in_second, grad_in, rate_matrix, decay_matrix)
    out_new = adamw(out_weight, out_first, out_second, grad_out.T, rate_matrix, decay_matrix)
    gu_new = adamw(gu_weight, gu_first, gu_second, grad_gu, rate_matrix, decay_matrix)
    down_new = adamw(down_weight, down_first, down_second, grad_dn.T, rate_matrix, decay_matrix)
    conv_new = adamw(conv_weight, conv_first, conv_second, conv_grad, rate_small, 0.0)
    gains_new = adamw(norm_gains, gains_first, gains_second, gains_grad, rate_small, 0.0)
    return (
        mixed.reshape(tokens.shape).astype(f32),
        tg.reshape(tokens.shape).astype(f32),
        *in_new,
        *out_new,
        *gu_new,
        *down_new,
        *conv_new,
        *gains_new,
    )


def solution(mesh):
    rows = P("dp", "seq", None)
    stack = P(None, ("dp", "seq"), "mp")
    flat = P("mp", ("dp", "seq"))
    thin = P(None, ("dp", "seq"))
    groups = (stack,) * 3 + (flat,) * 3 + (stack,) * 3 + (flat,) * 3 + (thin,) * 6
    return jax.shard_map(
        local,
        mesh=mesh,
        in_specs=(rows, rows) + groups,
        out_specs=(rows, rows) + groups,
        check_vma=False,
    )
```

time: 882 us -> 145 us (0.16)
  waiting for transfers between devices: 683 us -> 0 us
  Pallas kernels: 0 us -> 128 us
  blocking collectives: 80 us -> 0 us
  matrix products: 52.3 us -> 0 us
  other arithmetic: 37.9 us -> 10.1 us
  between operations: 14.8 us -> 0.86 us
    reduce_scatter x4 -> x0, waiting for transfers between devices: 311 us -> none  [the longest x1 85 us: local(): lax.psum_scatter(grad_gu.astype(jnp.bfloat16), ('dp', 'seq'), scatter_dim...]
    psum x3 -> x0, waiting for transfers between devices: 152 us -> none  [the longest x1 56.6 us: local(): lax.psum(jnp.dot(hidden, down_full, preferred_element_type=f32).astype(jn...]
    unnamed x14 -> x0, waiting for transfers between devices: 135 us -> none
    pallas_call x0 -> x1, Pallas kernels: none -> 128 us  [local(): pl.pallas_call(kernel, out_shape=(shape((4, CHUNK, D), bf16), shape((4, C...]
    all_gather x3 -> x0, waiting for transfers between devices: 84 us -> none  [the longest x1 45.4 us: local(): lax.all_gather(gu_weight.astype(bf16), ('dp', 'seq'), axis=1, tiled=True)]
    all_gather x3 -> x0, blocking collectives: 68.9 us -> none  [the longest x1 23.2 us: local(): lax.all_gather(out_weight.astype(bf16), ('dp', 'seq'), axis=1, tiled=True)]
    dot_general x21 -> x0, matrix products: 52.3 us -> none  [the longest x1 6.82 us: local(): jnp.einsum('td,fd->tf', up_low, down_full, preferred_element_type=f32)]
    psum x1 -> x0, blocking collectives: 11.2 us -> none  [local(): lax.psum(taps_padded.astype(jnp.bfloat16), 'mp').astype(jnp.float32)]
  transfers between devices with their start and end apart: 14 -> 0, of which waited for: 12 -> 0; matrix products, arithmetic and copies ran while one was open for 7% -> 0% of each run, Pallas kernels for 0% -> 0%
where the time goes in v1:
time: 145 us; the launch traced here: 143 us
  Pallas kernels  128 us (88%)
  other arithmetic  10.1 us (7%)
  local copies, waits for them, and re-layouts  3.61 us (2%)
    pallas_call x1, Pallas kernels, local(): pl.pallas_call(kernel, out_shape=(shape((4, CHUNK, D), bf16), shape((4, C...  128 us
    sub x6, other arithmetic, adamw(): master - rate * (moment_hat / (jnp.sqrt(square_hat) + eps_adam) + decay *...  5.96 us
    convert_element_type x1, other arithmetic, local(): tg.reshape(tokens.shape).astype(f32)  4.11 us
    unnamed x46, local copies, waits for them, and re-layouts  3.61 us

profile of v1, /device:TPU:0, one launch (start us, length us, event | category | flops | bytes accessed | tf_op | source)
XLA Modules:
  0.0 142.6 jit_solution(11835429161767902500)
XLA Ops:
  0.7 2.0 %copy.41.w_dn = f32[1152,32]{1,0:T(8,128)} copy(f32[1152,32]{0,1:T(8,128)} %param.31) | data formatting | bytes 294912 | tf_op args[11]
  2.6 1.5 %copy.40.w_out = f32[256,32]{1,0:T(8,128)} copy(f32[256,32]{0,1:T(8,128)} %param.25) | data formatting | bytes 65536 | tf_op args[5]
  4.2 0.0 copy-start.20
  4.2 0.0 copy-start.21
  4.2 128.1 %block_step.1 = (bf16[4,128,1024]{2,1,0:T(8,128)(2,1)}, bf16[4,128,1024]{2,1,0:T(8,128)(2,1)}, f32[3,32,256]{2,1,0:T(8,128)}, f32[32,256]{1,0:T(8,128)}, f32[2,3...) custom-call(f32[512,1024]{1,0:T(8,128)} %bitcast.23, f32[512,1024]{1,0:T(8,128)} %bitcast.24, ...), custom_call_target="tpu_custom_call" | custom-call | tf_op jit(solution)/shard_map/block_step/pallas_call | solution.py:560
  132.3 1.4 multiply_subtract_fusion.4
  133.7 0.0 copy-done.21
  133.7 1.3 multiply_subtract_fusion.5
  135.0 4.1 %bitcast_convert_fusion = (f32[1,512,1024]{2,1,0:T(8,128)}, f32[1,512,1024]{2,1,0:T(8,128)}) fusion(bf16[1,512,1024]{2,1,0:T(8,128)(2,1)} %bitcast.26, bf16[1,512,1024]{2,1,0:T(8,128)(2,1)} %bitcast.25), kind=kLoop, calls=%fused_computation | loop fusion | flops 1048576 | bytes 6291456 | tf_op jit(solution)/shard_map/convert_element_type | solution.py:638
  139.2 0.0 copy-start.2
  139.2 0.0 copy-start.10
  139.2 0.0 copy-start.11
  139.2 0.0 copy-start.9
  139.2 0.0 copy-start.13
  139.2 0.0 copy-start.14
  139.3 1.0 multiply_subtract_fusion
  140.3 0.0 copy-done.6
  140.3 0.0 copy-done.8
  140.4 0.8 multiply_subtract_fusion.1
  141.2 0.0 copy-done.10
  141.2 0.7 multiply_subtract_fusion.2
  142.0 0.0 copy-done.14
  142.0 0.0 copy-done.15
  142.0 0.7 multiply_subtract_fusion.3
  (30 shorter events, 0.1 us)
Async XLA Ops:
  4.1 128.2 %copy-start.16 = (f32[3,32]{1,0:T(4,128)S(1)}, f32[3,32]{1,0:T(4,128)}, u32[]{:S(2)}) copy-start(f32[3,32]{1,0:T(4,128)} %w_conv.1) | copy-start | bytes 1156
  4.1 128.2 %copy-start.18 = (f32[3,32]{1,0:T(4,128)S(1)}, f32[3,32]{1,0:T(4,128)}, u32[]{:S(2)}) copy-start(f32[3,32]{1,0:T(4,128)} %param.35) | copy-start | bytes 1156
  4.1 128.2 %copy-start.19 = (f32[3,32]{1,0:T(4,128)S(1)}, f32[3,32]{1,0:T(4,128)}, u32[]{:S(2)}) copy-start(f32[3,32]{1,0:T(4,128)} %param.36) | copy-start | bytes 1156
  4.1 129.5 %copy-start.17 = (f32[2,32]{1,0:T(2,128)S(1)}, f32[2,32]{1,0:T(2,128)}, u32[]{:S(2)}) copy-start(f32[2,32]{1,0:T(2,128)} %w_gain.1) | copy-start | bytes 772
  4.2 129.5 %copy-start.20 = (f32[2,32]{1,0:T(2,128)S(1)}, f32[2,32]{1,0:T(2,128)}, u32[]{:S(2)}) copy-start(f32[2,32]{1,0:T(2,128)} %param.38) | copy-start | bytes 772
  4.2 129.5 %copy-start.21 = (f32[2,32]{1,0:T(2,128)S(1)}, f32[2,32]{1,0:T(2,128)}, u32[]{:S(2)}) copy-start(f32[2,32]{1,0:T(2,128)} %param.39) | copy-start | bytes 772
  135.0 4.2 %copy-start = (f32[2,32,1152]{2,1,0:T(8,128)S(1)}, f32[2,32,1152]{2,1,0:T(8,128)}, u32[]{:S(2)}) copy-start(f32[2,32,1152]{2,1,0:T(8,128)} %w_gu.1) | copy-start | bytes 884740
  135.0 4.2 %copy-start.3 = (f32[2,32,1152]{2,1,0:T(8,128)S(1)}, f32[2,32,1152]{2,1,0:T(8,128)}, u32[]{:S(2)}) copy-start(f32[2,32,1152]{2,1,0:T(8,128)} %param.29) | copy-start | bytes 884740
  135.0 4.2 %copy-start.4 = (f32[2,32,1152]{2,1,0:T(8,128)S(1)}, f32[2,32,1152]{2,1,0:T(8,128)}, u32[]{:S(2)}) copy-start(f32[2,32,1152]{2,1,0:T(8,128)} %param.30) | copy-start | bytes 884740
  135.0 4.3 %copy-start.5 = (f32[2,32,1152]{2,1,0:T(8,128)S(1)}, f32[2,32,1152]{2,1,0:T(8,128)}, u32[]{:S(2)}) copy-start(f32[2,32,1152]{2,1,0:T(8,128)} %get-tuple-element.31) | copy-start | bytes 884740
  139.1 1.2 copy-start.1
  139.1 1.2 copy-start.6
  139.1 1.2 copy-start.7
  139.2 1.2 copy-start.8
  139.2 2.0 %copy-start.2 = (f32[3,32,256]{2,1,0:T(8,128)S(1)}, f32[3,32,256]{2,1,0:T(8,128)}, u32[]{:S(2)}) copy-start(f32[3,32,256]{2,1,0:T(8,128)} %w_in.1) | copy-start | bytes 294916
  139.2 2.0 %copy-start.10 = (f32[3,32,256]{2,1,0:T(8,128)S(1)}, f32[3,32,256]{2,1,0:T(8,128)}, u32[]{:S(2)}) copy-start(f32[3,32,256]{2,1,0:T(8,128)} %param.23) | copy-start | bytes 294916
  139.2 2.0 %copy-start.11 = (f32[3,32,256]{2,1,0:T(8,128)S(1)}, f32[3,32,256]{2,1,0:T(8,128)}, u32[]{:S(2)}) copy-start(f32[3,32,256]{2,1,0:T(8,128)} %param.24) | copy-start | bytes 294916
  139.2 2.0 %copy-start.12 = (f32[3,32,256]{2,1,0:T(8,128)S(1)}, f32[3,32,256]{2,1,0:T(8,128)}, u32[]{:S(2)}) copy-start(f32[3,32,256]{2,1,0:T(8,128)} %get-tuple-element.29) | copy-start | bytes 294916
  139.2 2.8 %copy-start.9 = (f32[256,32]{0,1:T(8,128)S(1)}, f32[256,32]{0,1:T(8,128)}, u32[]{:S(2)}) copy-start(f32[256,32]{0,1:T(8,128)} %param.25) | copy-start | bytes 98308
  139.2 2.8 %copy-start.13 = (f32[256,32]{0,1:T(8,128)S(1)}, f32[256,32]{0,1:T(8,128)}, u32[]{:S(2)}) copy-start(f32[256,32]{0,1:T(8,128)} %param.26) | copy-start | bytes 98308
  139.2 2.7 %copy-start.14 = (f32[256,32]{0,1:T(8,128)S(1)}, f32[256,32]{0,1:T(8,128)}, u32[]{:S(2)}) copy-start(f32[256,32]{0,1:T(8,128)} %param.27) | copy-start | bytes 98308
  139.2 2.7 %copy-start.15 = (f32[32,256]{1,0:T(8,128)S(1)}, f32[32,256]{1,0:T(8,128)}, u32[]{:S(2)}) copy-start(f32[32,256]{1,0:T(8,128)} %get-tuple-element.30) | copy-start | bytes 98308

commit v2 on v1

--- a/solution.py
+++ b/solution.py
@@ -52,7 +52,7 @@
     return lax.dot_general(a, b, (((0,), (0,)), ((), ())), preferred_element_type=f32)
 
 
-N_SEMS = 128
+N_SEMS = 144
 
 
 def kernel(
@@ -138,6 +138,7 @@
 
     def send(src, dst, where):
         i = counter[0]
+        assert i < N_SEMS
         counter[0] += 1
         copy = pltpu.make_async_remote_copy(
             src, dst, ssem.at[i], rsem.at[i], device_id=where, device_id_type=MESH
@@ -163,7 +164,7 @@
 
     for k in range(3):
         W[z, x, c, :, CH * k : CH * k + CH] = w_in[k].astype(bf16)
-    W[z, x, c, :, OUT0:SM0] = w_out[...].T.astype(bf16)
+    W[z, x, c, :, OUT0:SM0] = w_out[...].astype(bf16)
     square[...] = jnp.zeros((128, 128), f32)
     square[0:3, 0:32] = w_conv[...]
     square[3:5, 0:32] = w_gain[...]
@@ -172,7 +173,7 @@
         for k in range(2):
             at = GU0 + 256 * t + 128 * k
             W[z, x, c, :, at : at + 128] = w_gu[k, :, 128 * t : 128 * t + 128].astype(bf16)
-    W[z, x, c, :, DN0:COLS] = w_dn[...].T.astype(bf16)
+    W[z, x, c, :, DN0:COLS] = w_dn[...].astype(bf16)
     pl.semaphore_wait(barrier, len(peers))
 
     def ag_one(lo, mid, hi):
@@ -187,9 +188,23 @@
         a, b = pl.ds(lo, mid - lo), pl.ds(mid, hi - mid)
         src_a, src_b = W.at[z, :, c, :, a], W.at[:, x, c, :, b]
         arrived(copies[0])
-        first = [send(src_a, src_a, to_z(s)) for s in (1, 3, 2)]
+        first = [send(src_a, src_a, to_z(s)) for s in (1, 3)]
         arrived(copies[1])
-        return first + [send(src_b, src_b, to_x(s)) for s in (1, 3, 2)]
+        return first, [send(src_b, src_b, to_x(s)) for s in (1, 3)]
+
+    def ag_pass(copies, lo, mid, hi):
+        a, b = pl.ds(lo, mid - lo), pl.ds(mid, hi - mid)
+        low, high = pl.ds(0, 2), pl.ds(2, 2)
+        out = []
+        for s, half in ((1, low), (3, high)):
+            i = 0 if s == 1 else 1
+            arrived([copies[0][i]])
+            src = W.at[near(z, 4 - s), half, c, :, a]
+            out += [send(src, src, to_z(s))]
+            arrived([copies[1][i]])
+            src = W.at[half, near(x, 4 - s), c, :, b]
+            out += [send(src, src, to_x(s))]
+        return out
 
     def ag_three(copies, lo, hi):
         arrived(copies)
@@ -207,8 +222,9 @@
     ag0 = ag_two(ag0, *g0)
     ag1 = ag_one(*g1)
     ag2 = ag_one(*g2)
+    ag0 = ag_pass(ag0, *g0)
+    ag1 = ag_two(ag1, *g1)
     ag0 = ag_three(ag0, IN0, GU0)
-    ag1 = ag_two(ag1, *g1)
     ag2 = ag_two(ag2, *g2)
     arrived(ag0)
 
@@ -260,6 +276,53 @@
             return [send(PY.at[which, step - 1], RY.at[which, step - 1], to_y(step))]
         return []
 
+    half = CHUNK // 2
+    low_half, high_half = pl.ds(0, half), pl.ds(half, half)
+
+    def part_of(which, slot, rows, where):
+        return send(PY.at[which, slot, rows], RY.at[which, slot, rows], where)
+
+    def rs_y(which, source, lo, n):
+        def block_of(step):
+            return source[chunk_rows(step)]
+
+        for step in (2, 1, 3, 0):
+            values = block_of(step)
+            for block in range(4):
+                part = dot_nt(values, weight_rows(block, lo, n))
+                cols = slice(block * 256, block * 256 + 256)
+                if step == 0:
+                    OWN[which, :, cols] = part
+                else:
+                    PY[which, step - 1, :, cols] = part.astype(bf16)
+            if step == 2:
+                relay = (
+                    part_of(which, 1, low_half, to_y(1)),
+                    part_of(which, 1, high_half, to_y(3)),
+                )
+            elif step == 1:
+                direct = [part_of(which, 0, high_half, to_y(1))]
+            elif step == 3:
+                direct += [part_of(which, 2, low_half, to_y(3))]
+        return relay, direct
+
+    def rs_y_pass(which, state):
+        relay, direct = state
+        out = list(direct)
+        for k, (slot, rows, where) in enumerate(
+            ((0, slice(0, half), to_y(1)), (2, slice(half, CHUNK), to_y(3)))
+        ):
+            arrived([relay[k]])
+            PY[which, slot, rows] = (
+                PY[which, slot, rows].astype(f32) + RY[which, 1, rows].astype(f32)
+            ).astype(bf16)
+            out += [part_of(which, slot, low_half if k == 0 else high_half, where)]
+        return out
+
+    def summed_relayed(which, copies):
+        arrived(copies)
+        return OWN[which] + RY[which, 0].astype(f32) + RY[which, 2].astype(f32)
+
     def summed(which, copies):
         arrived(copies)
         return (
@@ -273,7 +336,6 @@
         return (send(src, slot(y), to_y(1)), send(src, slot(y), to_y(3)))
 
     def ag_y_pass(copies, slot):
-        half = CHUNK // 2
         arrived(copies[:1])
         left = slot(near(y, 3)).at[pl.ds(0, half)]
         out = [send(left, left, to_y(1))]
@@ -281,15 +343,15 @@
         right = slot(near(y, 1)).at[pl.ds(half, half)]
         return out + [send(right, right, to_y(3))]
 
-    rs = []
-    for step in (2, 1, 3, 0):
-        rs += partial(0, step, gated[chunk_rows(step)], OUT0, CH)
-
+    rs = rs_y(0, gated, OUT0, CH)
+    ag1 = ag_pass(ag1, *g1)
+    rs = rs_y_pass(0, rs)
+    ag2 = ag_pass(ag2, *g2)
     ag1 = ag_three(ag1, GU0, DN0)
     ag2 = ag_three(ag2, DN0, COLS)
 
     own_rows = chunk_rows(0)
-    resid = tok[own_rows] + summed(0, rs)
+    resid = tok[own_rows] + summed_relayed(0, rs)
     res_s[...] = resid
     act2[y] = (resid * rms_scale(resid) * gain_two).astype(bf16)
     def act2_slot(i):
@@ -398,10 +460,8 @@
         )
 
     gi = (IN0, 512, SM0)
-    weight_grad(
-        lambda i: act2[:, :, i * 256 : i * 256 + 256].reshape(ROWS, 256), GG, GU0, 2 * FF
-    )
-    r_gu = rs_core(GU0, DN0)
+    gi = (IN0, 512, SM0)
+    rs_ffn = rs_y(2, hid, DN0, FF)
 
     back_two = summed(1, rs)
     resid = res_s[...]
@@ -421,14 +481,15 @@
     ag_rlow = ag_y(rlow.at[y], rlow_slot)
     OWN[1] = grad_resid
 
+    weight_grad(
+        lambda i: act2[:, :, i * 256 : i * 256 + 256].reshape(ROWS, 256), GG, GU0, 2 * FF
+    )
+    r_gu = rs_core(GU0, DN0)
+    ag_rlow = ag_y_pass(ag_rlow, rlow_slot)
+    rs_ffn = rs_y_pass(2, rs_ffn)
     weight_grad(lambda i: ulow[:, i * 256 : i * 256 + 256], hid, DN0, FF)
     r_dn = rs_core(DN0, COLS)
-    rs_ffn = partial(2, 2, hid[chunk_rows(2)], DN0, FF)
     r_gu = rs_one(r_gu, *g1)
-    ag_rlow = ag_y_pass(ag_rlow, rlow_slot)
-    for step in (1, 3, 0):
-        rs_ffn += partial(2, step, hid[chunk_rows(step)], DN0, FF)
-    r_dn = rs_one(r_dn, *g2)
 
     arrived(ag_rlow)
     low = rlow[...].reshape(ROWS, D)
@@ -450,16 +511,13 @@
     GB[:, 0:CH] = (grad_mixed * x_s[...]).astype(bf16)
     GB[:, 2 * CH : 3 * CH] = (grad_mixed * b_s[...]).astype(bf16)
 
-    rs = []
-    for step in (2, 1, 3, 0):
-        rs += partial(3, step, GB[chunk_rows(step)], IN0, 3 * CH)
-
+    rs = rs_y(3, GB, IN0, 3 * CH)
     weight_grad(lambda i: act1[16:, i * 256 : i * 256 + 256], GB, IN0, 3 * CH)
     r_in = rs_core(IN0, SM0)
-    r_gu = rs_two(r_gu, *g1)
-    r_dn = rs_two(r_dn, *g2)
-
-    mixrow[...] = (res_s[...] + summed(2, rs_ffn)).astype(bf16)
+    r_dn = rs_one(r_dn, *g2)
+    rs = rs_y_pass(3, rs)
+
+    mixrow[...] = (res_s[...] + summed_relayed(2, rs_ffn)).astype(bf16)
 
     def mixed_slot(i):
         return mixed_o.at[i]
@@ -467,9 +525,10 @@
     ag_mixed = ag_y(mixrow, mixed_slot)
     local_mixed = pltpu.make_async_copy(mixrow, mixed_o.at[y], lsem.at[0])
     local_mixed.start()
+    r_gu = rs_two(r_gu, *g1)
     r_in = rs_one(r_in, *gi)
 
-    back_one = summed(3, rs)
+    back_one = summed_relayed(3, rs)
     own_tok = tok[own_rows]
     scale_one = rms_scale(own_tok)
     normed = own_tok * scale_one
@@ -489,6 +548,7 @@
 
     sm = [send(SM.at[0], SMR.at[0], to_core)]
     ag_mixed = ag_y_pass(ag_mixed, mixed_slot)
+    r_dn = rs_two(r_dn, *g2)
     arrived(sm)
     SM[1] = SM[0] + SMR[0]
     sm = [send(SM.at[1], SMR.at[s], to_x(s)) for s in (1, 3, 2)]
@@ -522,7 +582,14 @@
     def term(j):
         return SMR[7 + lax.rem(y - j + 4, 4)]
 
-    small_o[...] = ((term(0) + term(1)) + term(2)) + term(3)
+    shard_at = z * 8 + seq
+    SMR[0] = ((term(0) + term(1)) + term(2)) + term(3)
+    four = SMR[0, :, pl.ds(pl.multiple_of(shard_at // 4 * 128, 128), 128)]
+    place = lax.rem(shard_at, 4)
+    mine = four[:, 0:32]
+    for k in range(1, 4):
+        mine = jnp.where(place == k, four[:, 32 * k : 32 * k + 32], mine)
+    small_o[...] = mine
 
     arrived(ag_mixed)
     arrived(ag_tg)
@@ -530,6 +597,19 @@
     local_tg.wait()
     for copy in pending:
         copy.wait_send()
+
+
+def finish(*refs):
+    refs[25][...] = refs[0][...].astype(f32)
+    refs[26][...] = refs[1][...].astype(f32)
+    small = refs[6][...]
+    grads = [ref[...] for ref in refs[2:6]] + [small[0:3], small[3:5]]
+    for k, grad in enumerate(grads):
+        rate, decay = (rate_matrix, decay_matrix) if k < 4 else (rate_small, 0.0)
+        group = refs[7 + 3 * k : 10 + 3 * k]
+        new = adamw(*(ref[...] for ref in group), grad, rate, decay)
+        for ref, value in zip(refs[27 + 3 * k : 30 + 3 * k], new):
+            ref[...] = value
 
 
 def local(
@@ -566,7 +646,7 @@
             shape((32, CH), f32),
             shape((2, 32, FF), f32),
             shape((32, FF), f32),
-            shape((8, D), f32),
+            shape((8, 32), f32),
         ),
         in_specs=[hbm] * 2 + [vmem] * 6,
         out_specs=(hbm, hbm, vmem, vmem, vmem, vmem, vmem),
@@ -618,30 +698,50 @@
         tokens.reshape(ROWS, D),
         cotangent.reshape(ROWS, D),
         in_weight,
-        out_weight,
+        out_weight.T,
         gu_weight,
-        down_weight,
+        down_weight.T,
         conv_weight,
         norm_gains,
     )
-    here = (lax.axis_index("dp") * 8 + lax.axis_index("seq")) * 32
-    conv_grad = lax.dynamic_slice(grad_small, (0, here), (3, 32))
-    gains_grad = lax.dynamic_slice(grad_small, (3, here), (2, 32))
-    in_new = adamw(in_weight, in_first, in_second, grad_in, rate_matrix, decay_matrix)
-    out_new = adamw(out_weight, out_first, out_second, grad_out.T, rate_matrix, decay_matrix)
-    gu_new = adamw(gu_weight, gu_first, gu_second, grad_gu, rate_matrix, decay_matrix)
-    down_new = adamw(down_weight, down_first, down_second, grad_dn.T, rate_matrix, decay_matrix)
-    conv_new = adamw(conv_weight, conv_first, conv_second, conv_grad, rate_small, 0.0)
-    gains_new = adamw(norm_gains, gains_first, gains_second, gains_grad, rate_small, 0.0)
+    params = (
+        (in_weight, in_first, in_second),
+        (out_weight.T, out_first.T, out_second.T),
+        (gu_weight, gu_first, gu_second),
+        (down_weight.T, down_first.T, down_second.T),
+        (conv_weight, conv_first, conv_second),
+        (norm_gains, gains_first, gains_second),
+    )
+    grads = (grad_in, grad_out, grad_gu, grad_dn, grad_small)
+    big = pl.BlockSpec((CHUNK, D), lambda i: (i, 0))
+
+    def rows_of(array):
+        if array.ndim == 3:
+            return pl.BlockSpec((array.shape[0], 8, array.shape[2]), lambda i: (0, i, 0))
+        if array.shape[0] == 32:
+            return pl.BlockSpec((8, array.shape[1]), lambda i: (i, 0))
+        return pl.BlockSpec(array.shape, lambda i: (0, 0))
+
+    flat_params = [array for group in params for array in group]
+    specs = [rows_of(array) for array in flat_params]
+    done = pl.pallas_call(
+        finish,
+        grid=(4,),
+        out_shape=[shape((ROWS, D), f32)] * 2 + [shape(v.shape, f32) for v in flat_params],
+        in_specs=[big, big] + [rows_of(v) for v in grads] + specs,
+        out_specs=[big, big] + specs,
+        name="finish",
+    )(mixed.reshape(ROWS, D), tg.reshape(ROWS, D), *grads, *flat_params)
+    news = [done[2 + 3 * k : 5 + 3 * k] for k in range(6)]
     return (
-        mixed.reshape(tokens.shape).astype(f32),
-        tg.reshape(tokens.shape).astype(f32),
-        *in_new,
-        *out_new,
-        *gu_new,
-        *down_new,
-        *conv_new,
-        *gains_new,
+        done[0].reshape(tokens.shape),
+        done[1].reshape(tokens.shape),
+        *news[0],
+        *(v.T for v in news[1]),
+        *news[2],
+        *(v.T for v in news[3]),
+        *news[4],
+        *news[5],
     )
 
 

time: 145 us -> 135 us (0.931)
  other arithmetic: 10.1 us -> 0 us
  Pallas kernels: 128 us -> 133 us
  local copies, waits for them, and re-layouts: 3.61 us -> 0 us
    sub x6 -> x0, other arithmetic: 5.96 us -> none  [adamw(): master - rate * (moment_hat / (jnp.sqrt(square_hat) + eps_adam) + decay *...]
    pallas_call x0 -> x1, Pallas kernels: none -> 5.55 us  [local(): pl.pallas_call(finish, grid=(4,), out_shape=[shape((ROWS, D), f32)] * 2 +...]
    convert_element_type x1 -> x0, other arithmetic: 4.11 us -> none  [local(): tg.reshape(tokens.shape).astype(f32)]
    unnamed x46 -> x0, local copies, waits for them, and re-layouts: 3.61 us -> none
where the time goes in v2:
time: 135 us; the launch traced here: 133 us
  Pallas kernels  133 us (99%)
    pallas_call x1, Pallas kernels, local(): pl.pallas_call(kernel, out_shape=(shape((4, CHUNK, D), bf16), shape((4, C...  127 us
    pallas_call x1, Pallas kernels, local(): pl.pallas_call(finish, grid=(4,), out_shape=[shape((ROWS, D), f32)] * 2 +...  5.55 us

profile of v2, /device:TPU:0, one launch (start us, length us, event | category | flops | bytes accessed | tf_op | source)
XLA Modules:
  0.0 133.5 jit_solution(59281627619650676)
XLA Ops:
  0.7 127.1 %block_step.1 = (bf16[4,128,1024]{2,1,0:T(8,128)(2,1)}, bf16[4,128,1024]{2,1,0:T(8,128)(2,1)}, f32[3,32,256]{2,1,0:T(8,128)}, f32[32,256]{1,0:T(8,128)}, f32[2,3...) custom-call(f32[512,1024]{1,0:T(8,128)} %bitcast.18, f32[512,1024]{1,0:T(8,128)} %bitcast.19, ...), custom_call_target="tpu_custom_call" | custom-call | tf_op jit(solution)/shard_map/block_step/pallas_call | solution.py:640
  127.7 5.5 %finish.1 = (f32[512,1024]{1,0:T(8,128)}, f32[512,1024]{1,0:T(8,128)}, f32[3,32,256]{2,1,0:T(8,128)}, f32[3,32,256]{2,1,0:T(8,128)}, f32[3,32,256]{2,1,0:T(8,128...) custom-call(bf16[512,1024]{1,0:T(8,128)(2,1)} %bitcast.20, ...), custom_call_target="tpu_custom_call" | custom-call | tf_op jit(solution)/shard_map/finish/pallas_call | solution.py:727

commit v3 on v2

--- a/solution.py
+++ b/solution.py
@@ -24,7 +24,8 @@
 D = 1024
 CH = 256
 FF = 1152
-IN0, OUT0, SM0, GU0, DN0, COLS = 0, 768, 1024, 1152, 3456, 4608
+IN0, SM0, OUT0, GU0, DN0, COLS = 0, 768, 896, 1152, 3456, 4608
+GRAD_OUT0 = 768
 
 
 def adamw(master, first, second, grad, rate, decay):
@@ -52,7 +53,7 @@
     return lax.dot_general(a, b, (((0,), (0,)), ((), ())), preferred_element_type=f32)
 
 
-N_SEMS = 144
+N_SEMS = 176
 
 
 def kernel(
@@ -164,16 +165,11 @@
 
     for k in range(3):
         W[z, x, c, :, CH * k : CH * k + CH] = w_in[k].astype(bf16)
-    W[z, x, c, :, OUT0:SM0] = w_out[...].astype(bf16)
+    W[z, x, c, :, OUT0:GU0] = w_out[...].astype(bf16)
     square[...] = jnp.zeros((128, 128), f32)
     square[0:3, 0:32] = w_conv[...]
     square[3:5, 0:32] = w_gain[...]
-    W[z, x, c, :, SM0:GU0] = square[...].T[0:32].astype(bf16)
-    for t in range(9):
-        for k in range(2):
-            at = GU0 + 256 * t + 128 * k
-            W[z, x, c, :, at : at + 128] = w_gu[k, :, 128 * t : 128 * t + 128].astype(bf16)
-    W[z, x, c, :, DN0:COLS] = w_dn[...].astype(bf16)
+    W[z, x, c, :, SM0:OUT0] = square[...].T[0:32].astype(bf16)
     pl.semaphore_wait(barrier, len(peers))
 
     def ag_one(lo, mid, hi):
@@ -211,21 +207,54 @@
         src = W.at[:, :, c, :, pl.ds(lo, hi - lo)]
         return [send(src, src, to_core)]
 
-    g0 = (IN0, 640, GU0)
+    def ag_two_direct(copies, lo, mid, hi):
+        a, b = pl.ds(lo, mid - lo), pl.ds(mid, hi - mid)
+        src_a, src_b = W.at[z, :, c, :, a], W.at[:, x, c, :, b]
+        arrived(copies[0])
+        first = [send(src_a, src_a, to_z(s)) for s in (1, 3, 2)]
+        arrived(copies[1])
+        second = [send(src_b, src_b, to_x(s)) for s in (1, 3, 2)]
+        core = [send(src_a, src_a, to_core), send(src_b, src_b, to_core)]
+        return first, second, core
+
+    def ag_three_direct(copies, lo, mid, hi):
+        a, b = pl.ds(lo, mid - lo), pl.ds(mid, hi - mid)
+        first, second, core = copies
+        for k, s in enumerate((1, 3, 2)):
+            arrived([first[k]])
+            src = W.at[near(z, 4 - s), :, c, :, a]
+            core = core + [send(src, src, to_core)]
+            arrived([second[k]])
+            src = W.at[:, near(x, 4 - s), c, :, b]
+            core = core + [send(src, src, to_core)]
+        return core
+
+    g0 = (IN0, 512, OUT0)
+    go = (OUT0, OUT0 + 128, GU0)
     g1 = (GU0, GU0 + 1152, DN0)
     g2 = (DN0, DN0 + 640, COLS)
     ag0 = ag_one(*g0)
+    ago = ag_one(*go)
     halo = send(tok_h.at[pl.ds(ROWS - 16, 16)], htok, to_next)
+    for t in range(9):
+        for k in range(2):
+            at = GU0 + 256 * t + 128 * k
+            W[z, x, c, :, at : at + 128] = w_gu[k, :, 128 * t : 128 * t + 128].astype(bf16)
+    W[z, x, c, :, DN0:COLS] = w_dn[...].astype(bf16)
+    ag0 = ag_two_direct(ag0, *g0)
+    ago = ag_two_direct(ago, *go)
+    ag1 = ag_one(*g1)
+    ag2 = ag_one(*g2)
+    load_tok.wait()
+    for i in range(4):
+        v = tok[CHUNK * i : CHUNK * i + CHUNK]
+        OWN[i] = v * rms_scale(v)
+    ag0 = ag_three_direct(ag0, *g0)
+    ag1 = ag_two(ag1, *g1)
     load_cot.wait()
     for r in range(0, ROWS, 128):
         ulow[r : r + 128] = cot[r : r + 128].astype(bf16)
-    ag0 = ag_two(ag0, *g0)
-    ag1 = ag_one(*g1)
-    ag2 = ag_one(*g2)
-    ag0 = ag_pass(ag0, *g0)
-    ag1 = ag_two(ag1, *g1)
-    ag0 = ag_three(ag0, IN0, GU0)
-    ag2 = ag_two(ag2, *g2)
+    ago = ag_three_direct(ago, *go)
     arrived(ag0)
 
     def weights(lo, n):
@@ -241,14 +270,11 @@
     taps = smw[:, own_channels]
     tap0, tap1, tap2 = taps[0:1], taps[1:2], taps[2:3]
 
-    def first_norm(v):
-        return (v * rms_scale(v) * gain_one).astype(bf16)
-
-    load_tok.wait()
-    for r in range(0, ROWS, 128):
-        act1[r + 16 : r + 144] = first_norm(tok[r : r + 128])
+    for i in range(4):
+        act1[CHUNK * i + 16 : CHUNK * i + 144] = (OWN[i] * gain_one).astype(bf16)
     arrived([halo])
-    act1[0:16] = first_norm(htok[...])
+    v = htok[...]
+    act1[0:16] = (v * rms_scale(v) * gain_one).astype(bf16)
     bgate = dot_nn(act1[...], weights(0, CH))
     xvalue = dot_nn(act1[...], weights(2 * CH, CH))
     xext[...] = (bgate * xvalue).astype(bf16).astype(f32)
@@ -260,21 +286,26 @@
         tap0 * xext[14 : ROWS + 14] + tap1 * xext[15 : ROWS + 15] + tap2 * xext[16 : ROWS + 16]
     )
     gated[...] = (c_s[...] * conv_s[...]).astype(bf16)
+    arrived(ago)
 
     def chunk_rows(step):
         return pl.ds(pl.multiple_of(near(y, step) * CHUNK, CHUNK), CHUNK)
 
-    def partial(which, step, values, lo, n):
+    def partial(which, steps, values, lo, n):
         for block in range(4):
             part = dot_nt(values, weight_rows(block, lo, n))
             cols = slice(block * 256, block * 256 + 256)
-            if step == 0:
-                OWN[which, :, cols] = part
-            else:
-                PY[which, step - 1, :, cols] = part.astype(bf16)
-        if step:
-            return [send(PY.at[which, step - 1], RY.at[which, step - 1], to_y(step))]
-        return []
+            for k, step in enumerate(steps):
+                piece = part[CHUNK * k : CHUNK * k + CHUNK]
+                if step == 0:
+                    OWN[which, :, cols] = piece
+                else:
+                    PY[which, step - 1, :, cols] = piece.astype(bf16)
+        return [
+            send(PY.at[which, step - 1], RY.at[which, step - 1], to_y(step))
+            for step in steps
+            if step
+        ]
 
     half = CHUNK // 2
     low_half, high_half = pl.ds(0, half), pl.ds(half, half)
@@ -344,6 +375,7 @@
         return out + [send(right, right, to_y(3))]
 
     rs = rs_y(0, gated, OUT0, CH)
+    ag2 = ag_two(ag2, *g2)
     ag1 = ag_pass(ag1, *g1)
     rs = rs_y_pass(0, rs)
     ag2 = ag_pass(ag2, *g2)
@@ -370,27 +402,34 @@
             grad = gh[:, 128 * j : 128 * j + 128]
             sig = jax.nn.sigmoid(gate)
             swish = gate * sig
-            hid[rows, pl.ds(f_lo + 128 * j, 128)] = (swish * up).astype(bf16)
-            grad_gate = grad * up * sig * (1.0 + gate * (1.0 - sig))
-            GG[rows, pl.ds(2 * f_lo + 256 * j, 128)] = grad_gate.astype(bf16)
-            GG[rows, pl.ds(2 * f_lo + 256 * j + 128, 128)] = (grad * swish).astype(bf16)
+            hidden = (swish * up).astype(bf16)
+            grad_gate = (grad * up * sig * (1.0 + gate * (1.0 - sig))).astype(bf16)
+            grad_up = (grad * swish).astype(bf16)
+            for k, here in enumerate(rows):
+                piece = slice(CHUNK * k, CHUNK * k + CHUNK)
+                hid[here, pl.ds(f_lo + 128 * j, 128)] = hidden[piece]
+                GG[here, pl.ds(2 * f_lo + 256 * j, 128)] = grad_gate[piece]
+                GG[here, pl.ds(2 * f_lo + 256 * j + 128, 128)] = grad_up[piece]
+
+    def stacked(parts):
+        return parts[0] if len(parts) == 1 else jnp.concatenate(parts, axis=0)
 
     rs = []
-    for step in (0, 1, 3, 2):
-        if step == 1:
+    for steps in ((0,), (1, 3), (2,)):
+        if steps == (1, 3):
             ag_act2 = ag_y_pass(ag_act2, act2_slot)
-        if step == 2:
+        if steps == (2,):
             arrived(ag_act2)
-        rows = chunk_rows(step)
-        acts = act2[near(y, step)]
-        ups = ulow[rows]
+        rows = [chunk_rows(step) for step in steps]
+        acts = stacked([act2[near(y, step)] for step in steps])
+        ups = stacked([ulow[here] for here in rows])
 
         @pl.loop(0, 4)
         def _(t):
             ffn_part(acts, ups, rows, pl.multiple_of(t * 256, 256), 256)
 
         ffn_part(acts, ups, rows, 1024, 128)
-        rs += partial(1, step, GG[rows], GU0, 2 * FF)
+        rs += partial(1, steps, stacked([GG[here] for here in rows]), GU0, 2 * FF)
 
     def weight_grad(left, right, lo, n):
         for block in range(4):
@@ -459,8 +498,7 @@
             + RZ[2, :, cols].astype(f32)
         )
 
-    gi = (IN0, 512, SM0)
-    gi = (IN0, 512, SM0)
+    gi = (IN0, 512, 1024)
     rs_ffn = rs_y(2, hid, DN0, FF)
 
     back_two = summed(1, rs)
@@ -492,6 +530,15 @@
     r_gu = rs_one(r_gu, *g1)
 
     arrived(ag_rlow)
+
+    mixrow[...] = (res_s[...] + summed_relayed(2, rs_ffn)).astype(bf16)
+
+    def mixed_slot(i):
+        return mixed_o.at[i]
+
+    ag_mixed = ag_y(mixrow, mixed_slot)
+    local_mixed = pltpu.make_async_copy(mixrow, mixed_o.at[y], lsem.at[0])
+    local_mixed.start()
     low = rlow[...].reshape(ROWS, D)
     grad_gated = dot_nn(low, weights(OUT0, CH))
     gext[0:ROWS] = (grad_gated * c_s[...]).astype(bf16).astype(f32)
@@ -503,7 +550,7 @@
         row = jnp.sum(grad_conv * xext[14 + k : ROWS + 14 + k], axis=0, keepdims=True)
         SM[0, k : k + 1, own_channels] = row
     weight_grad(
-        lambda i: rlow[:, :, i * 256 : i * 256 + 256].reshape(ROWS, 256), gated, OUT0, CH
+        lambda i: rlow[:, :, i * 256 : i * 256 + 256].reshape(ROWS, 256), gated, GRAD_OUT0, CH
     )
     arrived([halo])
     gext[ROWS : ROWS + 8] = jnp.where(seq < 7, hb[...].astype(f32)[0:8], 0.0)
@@ -513,19 +560,11 @@
 
     rs = rs_y(3, GB, IN0, 3 * CH)
     weight_grad(lambda i: act1[16:, i * 256 : i * 256 + 256], GB, IN0, 3 * CH)
-    r_in = rs_core(IN0, SM0)
+    r_in = rs_core(IN0, 1024)
     r_dn = rs_one(r_dn, *g2)
     rs = rs_y_pass(3, rs)
-
-    mixrow[...] = (res_s[...] + summed_relayed(2, rs_ffn)).astype(bf16)
-
-    def mixed_slot(i):
-        return mixed_o.at[i]
-
-    ag_mixed = ag_y(mixrow, mixed_slot)
-    local_mixed = pltpu.make_async_copy(mixrow, mixed_o.at[y], lsem.at[0])
-    local_mixed.start()
-    r_gu = rs_two(r_gu, *g1)
+    ag_mixed = ag_y_pass(ag_mixed, mixed_slot)
+
     r_in = rs_one(r_in, *gi)
 
     back_one = summed_relayed(3, rs)
@@ -547,7 +586,7 @@
     local_tg.start()
 
     sm = [send(SM.at[0], SMR.at[0], to_core)]
-    ag_mixed = ag_y_pass(ag_mixed, mixed_slot)
+    r_gu = rs_two(r_gu, *g1)
     r_dn = rs_two(r_dn, *g2)
     arrived(sm)
     SM[1] = SM[0] + SMR[0]
@@ -575,7 +614,7 @@
     arrived(r_in)
     for k in range(3):
         g_in[k] = rs_end(IN0 + CH * k, CH, gi[1])
-    g_out[...] = rs_end(OUT0, CH, gi[1])
+    g_out[...] = rs_end(GRAD_OUT0, CH, gi[1])
 
     arrived(sm)
 

time: 135 us -> 136 us (level)
  Pallas kernels: 133 us -> 135 us
    pallas_call x1, Pallas kernels: 127 us -> 129 us  [local(): pl.pallas_call(kernel, out_shape=(shape((4, CHUNK, D), bf16), shape((4, C...]
where the time goes in v3:
time: 136 us
  Pallas kernels  135 us (99%)
    pallas_call x1, Pallas kernels, local(): pl.pallas_call(kernel, out_shape=(shape((4, CHUNK, D), bf16), shape((4, C...  129 us
    pallas_call x1, Pallas kernels, local(): pl.pallas_call(finish, grid=(4,), out_shape=[shape((ROWS, D), f32)] * 2 +...  5.55 us

profile of v3, /device:TPU:0, one launch (start us, length us, event | category | flops | bytes accessed | tf_op | source)
XLA Modules:
  0.0 135.7 jit_solution(8692590608695365924)
XLA Ops:
  0.7 129.3 %block_step.1 = (bf16[4,128,1024]{2,1,0:T(8,128)(2,1)}, bf16[4,128,1024]{2,1,0:T(8,128)(2,1)}, f32[3,32,256]{2,1,0:T(8,128)}, f32[32,256]{1,0:T(8,128)}, f32[2,3...) custom-call(f32[512,1024]{1,0:T(8,128)} %bitcast.18, f32[512,1024]{1,0:T(8,128)} %bitcast.19, ...), custom_call_target="tpu_custom_call" | custom-call | tf_op jit(solution)/shard_map/block_step/pallas_call | solution.py:679
  130.0 5.5 %finish.1 = (f32[512,1024]{1,0:T(8,128)}, f32[512,1024]{1,0:T(8,128)}, f32[3,32,256]{2,1,0:T(8,128)}, f32[3,32,256]{2,1,0:T(8,128)}, f32[3,32,256]{2,1,0:T(8,128...) custom-call(bf16[512,1024]{1,0:T(8,128)(2,1)} %bitcast.20, ...), custom_call_target="tpu_custom_call" | custom-call | tf_op jit(solution)/shard_map/finish/pallas_call | solution.py:766

commit v4 on v3

--- a/solution.py
+++ b/solution.py
@@ -53,7 +53,7 @@
     return lax.dot_general(a, b, (((0,), (0,)), ((), ())), preferred_element_type=f32)
 
 
-N_SEMS = 176
+N_SEMS = 192
 
 
 def kernel(
@@ -94,10 +94,10 @@
     conv_s,
     xext,
     gext,
-    mxb,
+    hlow,
     gated,
     GB,
-    hb,
+    c_after,
     smw,
     SM,
     SMR,
@@ -105,6 +105,7 @@
     RY,
     OWN,
     res_s,
+    own_tok,
     mixrow,
     tgrow,
     ssem,
@@ -153,7 +154,7 @@
             copy.wait_recv()
 
     barrier = pltpu.get_barrier_semaphore()
-    peers = [to_core, to_next, to_prev]
+    peers = [to_core, to_prev] + [(z, lax.rem(seq + 1, 8), k) for k in range(4)]
     for step in (1, 2, 3):
         peers += [to_x(step), to_z(step), to_y(step)]
     for peer in peers:
@@ -186,9 +187,11 @@
         arrived(copies[0])
         first = [send(src_a, src_a, to_z(s)) for s in (1, 3)]
         arrived(copies[1])
-        return first, [send(src_b, src_b, to_x(s)) for s in (1, 3)]
+        second = [send(src_b, src_b, to_x(s)) for s in (1, 3)]
+        return first, second, [send(src_a, src_a, to_core), send(src_b, src_b, to_core)]
 
     def ag_pass(copies, lo, mid, hi):
+        core = copies[2]
         a, b = pl.ds(lo, mid - lo), pl.ds(mid, hi - mid)
         low, high = pl.ds(0, 2), pl.ds(2, 2)
         out = []
@@ -200,12 +203,17 @@
             arrived([copies[1][i]])
             src = W.at[half, near(x, 4 - s), c, :, b]
             out += [send(src, src, to_x(s))]
-        return out
-
-    def ag_three(copies, lo, hi):
-        arrived(copies)
-        src = W.at[:, :, c, :, pl.ds(lo, hi - lo)]
-        return [send(src, src, to_core)]
+            src = W.at[near(z, 4 - s), :, c, :, a]
+            core = core + [send(src, src, to_core)]
+            src = W.at[:, near(x, 4 - s), c, :, b]
+            core = core + [send(src, src, to_core)]
+        return out, core
+
+    def ag_three(copies, lo, mid, hi):
+        a, b = pl.ds(lo, mid - lo), pl.ds(mid, hi - mid)
+        arrived(copies[0])
+        src_a, src_b = W.at[near(z, 2), :, c, :, a], W.at[:, near(x, 2), c, :, b]
+        return copies[1] + [send(src_a, src_a, to_core), send(src_b, src_b, to_core)]
 
     def ag_two_direct(copies, lo, mid, hi):
         a, b = pl.ds(lo, mid - lo), pl.ds(mid, hi - mid)
@@ -235,7 +243,10 @@
     g2 = (DN0, DN0 + 640, COLS)
     ag0 = ag_one(*g0)
     ago = ag_one(*go)
-    halo = send(tok_h.at[pl.ds(ROWS - 16, 16)], htok, to_next)
+    halo = [
+        send(tok_h.at[pl.ds(ROWS - 16, 16)], htok.at[0], to_next),
+        send(tok_h.at[pl.ds(0, 16)], htok.at[1], to_prev),
+    ]
     for t in range(9):
         for k in range(2):
             at = GU0 + 256 * t + 128 * k
@@ -246,11 +257,15 @@
     ag1 = ag_one(*g1)
     ag2 = ag_one(*g2)
     load_tok.wait()
+    mine = pl.ds(pl.multiple_of(y * CHUNK, CHUNK), CHUNK)
+    own_tok[...] = tok[mine]
     for i in range(4):
-        v = tok[CHUNK * i : CHUNK * i + CHUNK]
-        OWN[i] = v * rms_scale(v)
+        here = slice(CHUNK * i, CHUNK * i + CHUNK)
+        v = tok[here]
+        tok[here] = v * rms_scale(v)
     ag0 = ag_three_direct(ag0, *g0)
     ag1 = ag_two(ag1, *g1)
+    ag2 = ag_two(ag2, *g2)
     load_cot.wait()
     for r in range(0, ROWS, 128):
         ulow[r : r + 128] = cot[r : r + 128].astype(bf16)
@@ -271,17 +286,21 @@
     tap0, tap1, tap2 = taps[0:1], taps[1:2], taps[2:3]
 
     for i in range(4):
-        act1[CHUNK * i + 16 : CHUNK * i + 144] = (OWN[i] * gain_one).astype(bf16)
-    arrived([halo])
-    v = htok[...]
-    act1[0:16] = (v * rms_scale(v) * gain_one).astype(bf16)
-    bgate = dot_nn(act1[...], weights(0, CH))
-    xvalue = dot_nn(act1[...], weights(2 * CH, CH))
+        act1[CHUNK * i + 16 : CHUNK * i + 144] = (tok[CHUNK * i : CHUNK * i + CHUNK] * gain_one).astype(bf16)
+    arrived(halo)
+    for i in range(2):
+        v = htok[i]
+        at = i * (ROWS + 16)
+        act1[at : at + 16] = (v * rms_scale(v) * gain_one).astype(bf16)
+    bgate = dot_nn(act1[0 : ROWS + 16], weights(0, CH))
+    xvalue = dot_nn(act1[0 : ROWS + 16], weights(2 * CH, CH))
     xext[...] = (bgate * xvalue).astype(bf16).astype(f32)
     b_s[...] = bgate[16:]
     x_s[...] = xvalue[16:]
     xext[0:16] = jnp.where(seq > 0, xext[0:16], 0.0)
-    c_s[...] = dot_nn(act1[16:], weights(CH, CH))
+    cgate = dot_nn(act1[16:], weights(CH, CH))
+    c_s[...] = cgate[0:ROWS]
+    c_after[...] = cgate[ROWS:]
     conv_s[...] = (
         tap0 * xext[14 : ROWS + 14] + tap1 * xext[15 : ROWS + 15] + tap2 * xext[16 : ROWS + 16]
     )
@@ -313,7 +332,7 @@
     def part_of(which, slot, rows, where):
         return send(PY.at[which, slot, rows], RY.at[which, slot, rows], where)
 
-    def rs_y(which, source, lo, n):
+    def rs_y(which, source, lo, n, against=None):
         def block_of(step):
             return source[chunk_rows(step)]
 
@@ -322,6 +341,10 @@
             for block in range(4):
                 part = dot_nt(values, weight_rows(block, lo, n))
                 cols = slice(block * 256, block * 256 + 256)
+                if against is not None:
+                    SM[0, 3:4, cols] += jnp.sum(
+                        part * against[chunk_rows(step), cols], axis=0, keepdims=True
+                    )
                 if step == 0:
                     OWN[which, :, cols] = part
                 else:
@@ -375,15 +398,14 @@
         return out + [send(right, right, to_y(3))]
 
     rs = rs_y(0, gated, OUT0, CH)
-    ag2 = ag_two(ag2, *g2)
     ag1 = ag_pass(ag1, *g1)
+    ag2 = ag_pass(ag2, *g2)
     rs = rs_y_pass(0, rs)
-    ag2 = ag_pass(ag2, *g2)
-    ag1 = ag_three(ag1, GU0, DN0)
-    ag2 = ag_three(ag2, DN0, COLS)
+    ag1 = ag_three(ag1, *g1)
+    ag2 = ag_three(ag2, *g2)
 
     own_rows = chunk_rows(0)
-    resid = tok[own_rows] + summed_relayed(0, rs)
+    resid = own_tok[...] + summed_relayed(0, rs)
     res_s[...] = resid
     act2[y] = (resid * rms_scale(resid) * gain_two).astype(bf16)
     def act2_slot(i):
@@ -434,8 +456,8 @@
     def weight_grad(left, right, lo, n):
         for block in range(4):
             values = left(block)
-            for start in range(0, n, 384):
-                width = min(384, n - start)
+            for start in range(0, n, 256):
+                width = min(256, n - start)
                 part = dot_tn(values, right[:, pl.ds(start, width)])
                 G[block, :, :, :, pl.ds(lo + start, width)] = part.astype(bf16).reshape(
                     4, 2, 32, width
@@ -499,7 +521,10 @@
         )
 
     gi = (IN0, 512, 1024)
-    rs_ffn = rs_y(2, hid, DN0, FF)
+    weight_grad(
+        lambda i: act2[:, :, i * 256 : i * 256 + 256].reshape(ROWS, 256), GG, GU0, 2 * FF
+    )
+    r_gu = rs_core(GU0, DN0)
 
     back_two = summed(1, rs)
     resid = res_s[...]
@@ -516,62 +541,79 @@
     def rlow_slot(i):
         return rlow.at[i]
 
+    low_at = counter[0]
+    counter[0] += 4
+    low_halo = [
+        pltpu.make_async_remote_copy(
+            rlow.at[0, pl.ds(0, 16)],
+            hlow,
+            ssem.at[low_at + k],
+            rsem.at[low_at],
+            device_id=(z, lax.rem(seq + 7, 8), k),
+            device_id_type=MESH,
+        )
+        for k in range(4)
+    ]
+
+    @pl.when(y == 0)
+    def _():
+        for copy in low_halo:
+            copy.start()
+
     ag_rlow = ag_y(rlow.at[y], rlow_slot)
     OWN[1] = grad_resid
 
-    weight_grad(
-        lambda i: act2[:, :, i * 256 : i * 256 + 256].reshape(ROWS, 256), GG, GU0, 2 * FF
-    )
-    r_gu = rs_core(GU0, DN0)
+    rs_ffn = rs_y(2, hid, DN0, FF)
+    r_gu = rs_one(r_gu, *g1)
     ag_rlow = ag_y_pass(ag_rlow, rlow_slot)
-    rs_ffn = rs_y_pass(2, rs_ffn)
     weight_grad(lambda i: ulow[:, i * 256 : i * 256 + 256], hid, DN0, FF)
     r_dn = rs_core(DN0, COLS)
-    r_gu = rs_one(r_gu, *g1)
+    rs_ffn = rs_y_pass(2, rs_ffn)
 
     arrived(ag_rlow)
 
-    mixrow[...] = (res_s[...] + summed_relayed(2, rs_ffn)).astype(bf16)
-
-    def mixed_slot(i):
-        return mixed_o.at[i]
-
-    ag_mixed = ag_y(mixrow, mixed_slot)
-    local_mixed = pltpu.make_async_copy(mixrow, mixed_o.at[y], lsem.at[0])
-    local_mixed.start()
     low = rlow[...].reshape(ROWS, D)
     grad_gated = dot_nn(low, weights(OUT0, CH))
     gext[0:ROWS] = (grad_gated * c_s[...]).astype(bf16).astype(f32)
-    mxb[...] = gext[0:16].astype(bf16)
-    halo = send(mxb, hb, to_prev)
+    low_halo[0].wait_recv()
+    after = (dot_nn(hlow[...], weights(OUT0, CH)) * c_after[...]).astype(bf16).astype(f32)
+    gext[ROWS : ROWS + 8] = jnp.where(seq < 7, after[0:8], 0.0)
     GB[:, CH : 2 * CH] = (grad_gated * conv_s[...]).astype(bf16)
+    grad_mixed = tap2 * gext[0:ROWS] + tap1 * gext[1 : ROWS + 1] + tap0 * gext[2 : ROWS + 2]
+    GB[:, 0:CH] = (grad_mixed * x_s[...]).astype(bf16)
+    GB[:, 2 * CH : 3 * CH] = (grad_mixed * b_s[...]).astype(bf16)
+
+    rs = rs_y(3, GB, IN0, 3 * CH, tok)
     grad_conv = gext[0:ROWS]
     for k in range(3):
         row = jnp.sum(grad_conv * xext[14 + k : ROWS + 14 + k], axis=0, keepdims=True)
         SM[0, k : k + 1, own_channels] = row
+    sm = [send(SM.at[0], SMR.at[0], to_core)]
     weight_grad(
         lambda i: rlow[:, :, i * 256 : i * 256 + 256].reshape(ROWS, 256), gated, GRAD_OUT0, CH
     )
-    arrived([halo])
-    gext[ROWS : ROWS + 8] = jnp.where(seq < 7, hb[...].astype(f32)[0:8], 0.0)
-    grad_mixed = tap2 * gext[0:ROWS] + tap1 * gext[1 : ROWS + 1] + tap0 * gext[2 : ROWS + 2]
-    GB[:, 0:CH] = (grad_mixed * x_s[...]).astype(bf16)
-    GB[:, 2 * CH : 3 * CH] = (grad_mixed * b_s[...]).astype(bf16)
-
-    rs = rs_y(3, GB, IN0, 3 * CH)
-    weight_grad(lambda i: act1[16:, i * 256 : i * 256 + 256], GB, IN0, 3 * CH)
+    weight_grad(lambda i: act1[16 : ROWS + 16, i * 256 : i * 256 + 256], GB, IN0, 3 * CH)
+    arrived(sm)
+    SM[1] = SM[0] + SMR[0]
+    sm = [send(SM.at[1], SMR.at[s], to_x(s)) for s in (1, 3, 2)]
     r_in = rs_core(IN0, 1024)
     r_dn = rs_one(r_dn, *g2)
     rs = rs_y_pass(3, rs)
-    ag_mixed = ag_y_pass(ag_mixed, mixed_slot)
+
+    mixrow[...] = (res_s[...] + summed_relayed(2, rs_ffn)).astype(bf16)
+
+    def mixed_slot(i):
+        return mixed_o.at[i]
+
+    ag_mixed = ag_y(mixrow, mixed_slot)
+    local_mixed = pltpu.make_async_copy(mixrow, mixed_o.at[y], lsem.at[0])
+    local_mixed.start()
 
     r_in = rs_one(r_in, *gi)
 
     back_one = summed_relayed(3, rs)
-    own_tok = tok[own_rows]
-    scale_one = rms_scale(own_tok)
-    normed = own_tok * scale_one
-    SM[0, 3:4] = jnp.sum(back_one * normed, axis=0, keepdims=True)
+    scale_one = rms_scale(own_tok[...])
+    normed = tok[own_rows]
     scaled = back_one * gain_one
     tgrow[...] = (
         OWN[1]
@@ -585,31 +627,27 @@
     local_tg = pltpu.make_async_copy(tgrow, tg_o.at[y], lsem.at[1])
     local_tg.start()
 
-    sm = [send(SM.at[0], SMR.at[0], to_core)]
+    arrived(sm)
+    SM[2] = SM[1] + SMR[1] + SMR[2] + SMR[3]
+    sm = [send(SM.at[2], SMR.at[3 + s], to_z(s)) for s in (1, 3, 2)]
+    ag_mixed = ag_y_pass(ag_mixed, mixed_slot)
     r_gu = rs_two(r_gu, *g1)
     r_dn = rs_two(r_dn, *g2)
     arrived(sm)
-    SM[1] = SM[0] + SMR[0]
-    sm = [send(SM.at[1], SMR.at[s], to_x(s)) for s in (1, 3, 2)]
+    SMR[7] = SM[2] + SMR[4] + SMR[5] + SMR[6]
+    sm = [send(SMR.at[7], SMR.at[7 + s], to_y(s)) for s in (1, 3, 2)]
 
     arrived(r_dn)
     g_dn[:, 0:640] = rs_end(DN0, 640, g2[1])
     g_dn[:, 640:1152] = rs_end(DN0 + 640, 512, g2[1])
 
     r_in = rs_two(r_in, *gi)
-    arrived(sm)
-    SM[2] = SM[1] + SMR[1] + SMR[2] + SMR[3]
-    sm = [send(SM.at[2], SMR.at[3 + s], to_z(s)) for s in (1, 3, 2)]
 
     ag_tg = ag_y_pass(ag_tg, tg_slot)
     arrived(r_gu)
     for t in range(9):
         g_gu[0, :, 128 * t : 128 * t + 128] = rs_end(GU0 + 256 * t, 128, g1[1])
         g_gu[1, :, 128 * t : 128 * t + 128] = rs_end(GU0 + 256 * t + 128, 128, g1[1])
-
-    arrived(sm)
-    SMR[7] = SM[2] + SMR[4] + SMR[5] + SMR[6]
-    sm = [send(SMR.at[7], SMR.at[7 + s], to_y(s)) for s in (1, 3, 2)]
 
     arrived(r_in)
     for k in range(3):
@@ -636,6 +674,11 @@
     local_tg.wait()
     for copy in pending:
         copy.wait_send()
+
+    @pl.when(y == 0)
+    def _():
+        for copy in low_halo:
+            copy.wait_send()
 
 
 def finish(*refs):
@@ -692,7 +735,7 @@
         scratch_shapes=[
             pltpu.VMEM((ROWS, D), f32),
             pltpu.VMEM((ROWS, D), f32),
-            pltpu.VMEM((16, D), f32),
+            pltpu.VMEM((2, 16, D), f32),
             pltpu.VMEM((128, 128), f32),
             pltpu.VMEM((4, 4, 2, 32, COLS), bf16),
             pltpu.VMEM((4, 4, 2, 32, COLS), bf16),
@@ -700,7 +743,7 @@
             pltpu.VMEM((3, 4, 32, COLS), bf16),
             pltpu.VMEM((4, 32, COLS), bf16),
             pltpu.VMEM((3, 32, COLS), bf16),
-            pltpu.VMEM((ROWS + 16, D), bf16),
+            pltpu.VMEM((ROWS + 32, D), bf16),
             pltpu.VMEM((ROWS, D), bf16),
             pltpu.VMEM((4, CHUNK, D), bf16),
             pltpu.VMEM((4, CHUNK, D), bf16),
@@ -712,16 +755,17 @@
             pltpu.VMEM((ROWS, CH), f32),
             pltpu.VMEM((ROWS + 16, CH), f32),
             pltpu.VMEM((ROWS + 8, CH), f32),
-            pltpu.VMEM((16, CH), bf16),
+            pltpu.VMEM((16, D), bf16),
             pltpu.VMEM((ROWS, CH), bf16),
             pltpu.VMEM((ROWS, 3 * CH), bf16),
-            pltpu.VMEM((16, CH), bf16),
+            pltpu.VMEM((16, CH), f32),
             pltpu.VMEM((8, D), f32),
             pltpu.VMEM((3, 8, D), f32),
             pltpu.VMEM((11, 8, D), f32),
             pltpu.VMEM((4, 3, CHUNK, D), bf16),
             pltpu.VMEM((4, 3, CHUNK, D), bf16),
             pltpu.VMEM((4, CHUNK, D), f32),
+            pltpu.VMEM((CHUNK, D), f32),
             pltpu.VMEM((CHUNK, D), f32),
             pltpu.VMEM((CHUNK, D), bf16),
             pltpu.VMEM((CHUNK, D), bf16),

time: 136 us -> 126 us (0.926)
  Pallas kernels: 135 us -> 125 us
    pallas_call x1, Pallas kernels: 129 us -> 119 us  [local(): pl.pallas_call(kernel, out_shape=(shape((4, CHUNK, D), bf16), shape((4, C...]
where the time goes in v4:
time: 126 us; the launch traced here: 125 us
  Pallas kernels  125 us (99%)
    pallas_call x1, Pallas kernels, local(): pl.pallas_call(kernel, out_shape=(shape((4, CHUNK, D), bf16), shape((4, C...  119 us
    pallas_call x1, Pallas kernels, local(): pl.pallas_call(finish, grid=(4,), out_shape=[shape((ROWS, D), f32)] * 2 +...  5.55 us

profile of v4, /device:TPU:0, one launch (start us, length us, event | category | flops | bytes accessed | tf_op | source)
XLA Modules:
  0.0 125.4 jit_solution(3121783732799781907)
XLA Ops:
  0.7 119.0 %block_step.1 = (bf16[4,128,1024]{2,1,0:T(8,128)(2,1)}, bf16[4,128,1024]{2,1,0:T(8,128)(2,1)}, f32[3,32,256]{2,1,0:T(8,128)}, f32[32,256]{1,0:T(8,128)}, f32[2,3...) custom-call(f32[512,1024]{1,0:T(8,128)} %bitcast.18, f32[512,1024]{1,0:T(8,128)} %bitcast.19, ...), custom_call_target="tpu_custom_call" | custom-call | tf_op jit(solution)/shard_map/block_step/pallas_call | solution.py:722
  119.6 5.5 %finish.1 = (f32[512,1024]{1,0:T(8,128)}, f32[512,1024]{1,0:T(8,128)}, f32[3,32,256]{2,1,0:T(8,128)}, f32[3,32,256]{2,1,0:T(8,128)}, f32[3,32,256]{2,1,0:T(8,128...) custom-call(bf16[512,1024]{1,0:T(8,128)(2,1)} %bitcast.20, ...), custom_call_target="tpu_custom_call" | custom-call | tf_op jit(solution)/shard_map/finish/pallas_call | solution.py:810

commit v5 on v4

--- a/solution.py
+++ b/solution.py
@@ -572,6 +572,8 @@
 
     arrived(ag_rlow)
 
+    r_dn = rs_one(r_dn, *g2)
+
     low = rlow[...].reshape(ROWS, D)
     grad_gated = dot_nn(low, weights(OUT0, CH))
     gext[0:ROWS] = (grad_gated * c_s[...]).astype(bf16).astype(f32)
@@ -597,7 +599,6 @@
     SM[1] = SM[0] + SMR[0]
     sm = [send(SM.at[1], SMR.at[s], to_x(s)) for s in (1, 3, 2)]
     r_in = rs_core(IN0, 1024)
-    r_dn = rs_one(r_dn, *g2)
     rs = rs_y_pass(3, rs)
 
     mixrow[...] = (res_s[...] + summed_relayed(2, rs_ffn)).astype(bf16)

time: 126 us -> 123 us (0.976)
  Pallas kernels: 125 us -> 122 us
    pallas_call x1, Pallas kernels: 119 us -> 117 us  [local(): pl.pallas_call(kernel, out_shape=(shape((4, CHUNK, D), bf16), shape((4, C...]
where the time goes in v5:
time: 123 us
  Pallas kernels  122 us (99%)
    pallas_call x1, Pallas kernels, local(): pl.pallas_call(kernel, out_shape=(shape((4, CHUNK, D), bf16), shape((4, C...  117 us
    pallas_call x1, Pallas kernels, local(): pl.pallas_call(finish, grid=(4,), out_shape=[shape((ROWS, D), f32)] * 2 +...  5.55 us

profile of v5, /device:TPU:0, one launch (start us, length us, event | category | flops | bytes accessed | tf_op | source)
XLA Modules:
  0.0 123.1 jit_solution(13062470814898165046)
XLA Ops:
  0.7 116.7 %block_step.1 = (bf16[4,128,1024]{2,1,0:T(8,128)(2,1)}, bf16[4,128,1024]{2,1,0:T(8,128)(2,1)}, f32[3,32,256]{2,1,0:T(8,128)}, f32[32,256]{1,0:T(8,128)}, f32[2,3...) custom-call(f32[512,1024]{1,0:T(8,128)} %bitcast.18, f32[512,1024]{1,0:T(8,128)} %bitcast.19, ...), custom_call_target="tpu_custom_call" | custom-call | tf_op jit(solution)/shard_map/block_step/pallas_call | solution.py:723
  117.4 5.5 %finish.1 = (f32[512,1024]{1,0:T(8,128)}, f32[512,1024]{1,0:T(8,128)}, f32[3,32,256]{2,1,0:T(8,128)}, f32[3,32,256]{2,1,0:T(8,128)}, f32[3,32,256]{2,1,0:T(8,128...) custom-call(bf16[512,1024]{1,0:T(8,128)(2,1)} %bitcast.20, ...), custom_call_target="tpu_custom_call" | custom-call | tf_op jit(solution)/shard_map/finish/pallas_call | solution.py:811

commit v6 on v5

--- a/solution.py
+++ b/solution.py
@@ -590,6 +590,16 @@
     for k in range(3):
         row = jnp.sum(grad_conv * xext[14 + k : ROWS + 14 + k], axis=0, keepdims=True)
         SM[0, k : k + 1, own_channels] = row
+    mixrow[...] = (res_s[...] + summed_relayed(2, rs_ffn)).astype(bf16)
+
+    def mixed_slot(i):
+        return mixed_o.at[i]
+
+    ag_mixed = ag_y(mixrow, mixed_slot)
+    local_mixed = pltpu.make_async_copy(mixrow, mixed_o.at[y], lsem.at[0])
+    local_mixed.start()
+
+
     sm = [send(SM.at[0], SMR.at[0], to_core)]
     weight_grad(
         lambda i: rlow[:, :, i * 256 : i * 256 + 256].reshape(ROWS, 256), gated, GRAD_OUT0, CH
@@ -600,15 +610,6 @@
     sm = [send(SM.at[1], SMR.at[s], to_x(s)) for s in (1, 3, 2)]
     r_in = rs_core(IN0, 1024)
     rs = rs_y_pass(3, rs)
-
-    mixrow[...] = (res_s[...] + summed_relayed(2, rs_ffn)).astype(bf16)
-
-    def mixed_slot(i):
-        return mixed_o.at[i]
-
-    ag_mixed = ag_y(mixrow, mixed_slot)
-    local_mixed = pltpu.make_async_copy(mixrow, mixed_o.at[y], lsem.at[0])
-    local_mixed.start()
 
     r_in = rs_one(r_in, *gi)
 

time: 123 us -> 124 us (level); the launches traced: 123 us -> 122 us
  no operation moved by 1% of the time
where the time goes in v6:
time: 124 us; the launch traced here: 122 us
  Pallas kernels  122 us (98%)
    pallas_call x1, Pallas kernels, local(): pl.pallas_call(kernel, out_shape=(shape((4, CHUNK, D), bf16), shape((4, C...  116 us
    pallas_call x1, Pallas kernels, local(): pl.pallas_call(finish, grid=(4,), out_shape=[shape((ROWS, D), f32)] * 2 +...  5.55 us

profile of v6, /device:TPU:0, one launch (start us, length us, event | category | flops | bytes accessed | tf_op | source)
XLA Modules:
  0.0 122.5 jit_solution(12714420066164999645)
XLA Ops:
  0.7 116.1 %block_step.1 = (bf16[4,128,1024]{2,1,0:T(8,128)(2,1)}, bf16[4,128,1024]{2,1,0:T(8,128)(2,1)}, f32[3,32,256]{2,1,0:T(8,128)}, f32[32,256]{1,0:T(8,128)}, f32[2,3...) custom-call(f32[512,1024]{1,0:T(8,128)} %bitcast.18, f32[512,1024]{1,0:T(8,128)} %bitcast.19, ...), custom_call_target="tpu_custom_call" | custom-call | tf_op jit(solution)/shard_map/block_step/pallas_call | solution.py:724
  116.7 5.5 %finish.1 = (f32[512,1024]{1,0:T(8,128)}, f32[512,1024]{1,0:T(8,128)}, f32[3,32,256]{2,1,0:T(8,128)}, f32[3,32,256]{2,1,0:T(8,128)}, f32[3,32,256]{2,1,0:T(8,128...) custom-call(bf16[512,1024]{1,0:T(8,128)(2,1)} %bitcast.20, ...), custom_call_target="tpu_custom_call" | custom-call | tf_op jit(solution)/shard_map/finish/pallas_call | solution.py:812
